TPU v7x, 128 devices: a whole 4x4x4 slice. The times are simulated.
128 devices in a mesh: grp: 8 (over y_lo, x), tp: 16 (over z, y_hi, core).
Axes of the slice: x: 4, y: 4 (y_hi: 2, y_lo: 2; y = y_hi * 2 + y_lo), z: 4, core: 2. Of those that a mesh axis runs over, the one named last changes fastest.
Arguments:
- queries: bfloat16 [8, 2048, 8192], P('grp', None, 'tp'), may hold values from -400 to 400
- keys_values: bfloat16 [8, 2048, 2048], P('grp', 'tp'), may hold values from -6 to 6
- projector: bfloat16 [8192, 1024], P('tp'), may hold values from -1 to 1
- ownership: int32 [8], replicated, may hold values from 0 to 7, each once
- token_ids: int32 [16384], P(('grp', 'tp')), may hold values from 150143 to 152142
- student_input: bfloat16 [16384, 3584], P(('grp', 'tp')), may hold values from -24 to 24
- student_weight: bfloat16 [3584, 1024], P(('grp', 'tp')), may hold values from -0.09375 to 0.09375
- student_bias: bfloat16 [1024], P(('grp', 'tp')), may hold values from -3 to 3
Outputs:
- loss_value: float32 [], replicated
- weight_grad: float32 [3584, 1024], P(('grp', 'tp'))
- bias_grad: float32 [1024], P(('grp', 'tp'))
- input_grad: bfloat16 [16384, 3584], P(('grp', 'tp'))
Inputs may be any that keep to these rules, and one draw needn't show every extreme that they name: `ownership`: each number once.
All inputs are finite; a program needn't handle non-finite values.
Results may differ from a plain program's by a relative error of at most 0.019.
Values may be sent and summed in bfloat16 or wider, within the bound.
A program may use at most 128 MiB of HBM per device.

v0:
```python
import jax
import jax.numpy as jnp
from jax import lax
from jax.sharding import PartitionSpec as P

KV_HEADS = 8
HEAD_DIM = 128
TEXT_IDS = 151643


def attend(query_rows, key_rows, value_rows):
    length = query_rows.shape[0]
    block_rows = min(512, length)
    score_scale = HEAD_DIM ** (-0.5)
    outputs = []
    for first_row in range(0, length, block_rows):
        last_row = first_row + block_rows
        query_block = query_rows[first_row:last_row]
        scores = (
            jnp.einsum(
                "qhd,kd->hqk", query_block, key_rows[:last_row], preferred_element_type=jnp.float32
            )
            * score_scale
        )
        query_pos = first_row + jnp.arange(block_rows, dtype=jnp.int32)
        key_pos = jnp.arange(last_row, dtype=jnp.int32)
        causal = query_pos[:, None] >= key_pos[None, :]
        scores = jnp.where(causal[None], scores, -1e30)
        row_peak = jnp.max(scores, axis=2, keepdims=True)
        weights = jnp.exp(scores - row_peak)
        prob_rows = (weights / jnp.sum(weights, axis=2, keepdims=True)).astype(jnp.bfloat16)
        block_out = jnp.einsum(
            "hqk,kd->qhd", prob_rows, value_rows[:last_row], preferred_element_type=jnp.float32
        )
        outputs.append(block_out.astype(jnp.bfloat16).reshape(block_rows, -1))
    return jnp.concatenate(outputs, axis=0)


def on_device(
    queries,
    keys_values,
    projector,
    ownership,
    token_ids,
    student_input,
    student_weight,
    student_bias,
):
    stacked_rows = keys_values[0]
    rows_local = stacked_rows.shape[0]
    copies = lax.axis_size("tp") // KV_HEADS
    reshaped = stacked_rows.reshape(rows_local, 2, KV_HEADS, 1, HEAD_DIM)
    spread = jnp.broadcast_to(reshaped, (rows_local, 2, KV_HEADS, copies, HEAD_DIM))
    spread = spread.reshape(rows_local, 2, KV_HEADS * copies, HEAD_DIM)
    head_rows = lax.all_to_all(spread, "tp", split_axis=2, concat_axis=0, tiled=True)
    head_rows = head_rows.reshape(-1, 2, HEAD_DIM)
    key_rows = head_rows[:, 0]
    value_rows = head_rows[:, 1]
    query_rows = queries[0].reshape(queries.shape[1], -1, HEAD_DIM)
    attention = attend(query_rows, key_rows, value_rows)
    target_rows = lax.psum_scatter(
        jnp.dot(attention, projector, preferred_element_type=jnp.float32).astype(jnp.bfloat16),
        "tp",
        scatter_dimension=0,
        tiled=True,
    )
    groups = lax.axis_size("grp")
    pieces = target_rows.reshape(groups, rows_local // groups, -1)
    received = lax.all_to_all(pieces, "grp", split_axis=0, concat_axis=0, tiled=True)
    paired = jnp.take(received, ownership, axis=0).reshape(rows_local, -1)
    full_weight, full_bias = (
        lax.all_gather(student_weight, ("grp", "tp"), axis=0, tiled=True),
        lax.all_gather(student_bias, ("grp", "tp"), axis=0, tiled=True),
    )
    keep_mask = (token_ids < TEXT_IDS).astype(jnp.float32)[:, None]
    output = jnp.dot(
        student_input, full_weight, preferred_element_type=jnp.float32
    ) + full_bias.astype(jnp.float32)
    residual = keep_mask * (output - paired.astype(jnp.float32))
    loss_sum = lax.psum(jnp.sum(residual * residual), ("grp", "tp"))
    rows_total = student_input.shape[0] * lax.axis_size("grp") * lax.axis_size("tp")
    loss_value = loss_sum / (2.0 * rows_total)
    error_rows = residual.astype(jnp.bfloat16)
    weight_term = lax.dot_general(
        student_input, error_rows, (((0,), (0,)), ((), ())), preferred_element_type=jnp.float32
    )
    bias_term = jnp.sum(error_rows.astype(jnp.float32), axis=0)
    weight_grad, bias_grad = (
        lax.psum_scatter(weight_term, ("grp", "tp"), scatter_dimension=0, tiled=True),
        lax.psum_scatter(bias_term, ("grp", "tp"), scatter_dimension=0, tiled=True),
    )
    input_grad = lax.dot_general(
        error_rows, full_weight, (((1,), (1,)), ((), ())), preferred_element_type=jnp.float32
    )
    return (loss_value, weight_grad, bias_grad, input_grad.astype(jnp.bfloat16))


def solution(mesh):
    return jax.shard_map(
        on_device,
        mesh=mesh,
        in_specs=(
            P("grp", None, "tp"),
            P("grp", "tp", None),
            P("tp", None),
            P(),
            P(("grp", "tp")),
            P(("grp", "tp"), None),
            P(("grp", "tp"), None),
            P(("grp", "tp")),
        ),
        out_specs=(P(), P(("grp", "tp"), None), P(("grp", "tp")), P(("grp", "tp"), None)),
        check_vma=False,
    )
```

profile of v0, /device:TPU:1, one launch (start us, length us, event | category | flops | bytes accessed | tf_op | source)
XLA Modules:
  0.0 524.1 jit_solution(14108886430410499847)
XLA Ops:
  8.0 1.2 copy.81
  9.4 1.2 broadcast_in_dim.98
  10.6 9.5 %all-to-all-start = ((bf16[128,2,16,128]{3,0,1,2:T(8,128)(2,1)}), bf16[128,2,16,128]{3,0,1,2:T(8,128)(2,1)S(1)}, u32[]{:S(2)}, u32[]{:S(2)}) async-start(bf16[128,2,16,128]{3,0,1,2:T(8,128)(2,1)} %bitcast.1), calls=%async_computation | async-start | bytes 2097152 | tf_op jit(solution)/shard_map/all_to_all | solution.py:55
  20.2 2.9 fusion.58
  24.3 1.3 copy.79
  25.6 2.0 copy.78
  27.6 2.1 copy.77
  29.7 2.0 copy.80
  31.7 1.5 iota_compare_fusion.1
  33.2 1.9 iota_compare_fusion
  35.1 2.2 all-to-all-done
  38.4 1.8 fusion.44
  40.2 10.2 %fusion.60 = (f32[4,512]{1,0:T(4,128)S(1)}, f32[4,512,1536]{1,2,0:T(8,128)}) fusion(f32[1536,512,4]{1,0,2:T(8,128)S(1)} %fusion.44, pred[512,1536]{0,1:T(8,128)(4,1)} %iota_compare_fusion.1), kind=kOutput, calls=%fused_computation.97 | output fusion | flops 18875904 | bytes 25960448 | tf_op jit(solution)/shard_map/sub | solution.py:30
  50.4 7.5 %fusion.35 = bf16[4,512,128]{1,2,0:T(8,128)(2,1)} fusion(f32[4,512,1536]{1,2,0:T(8,128)} %get-tuple-element.27, f32[4,512]{1,0:T(4,128)S(1)} %get-tuple-element.26, bf16[2048,2,128]{2,0,1:T(8,128)(2,1)} %bitcast.158), kind=kOutput, calls=%fused_computation.53 | convolution fusion | flops 811859968 | bytes 13508608 | tf_op jit(solution)/shard_map/hqk,kd->qhd/dot_general | solution.py:32
  57.9 5.2 fusion.61
  63.1 5.6 %fusion.34 = bf16[4,512,128]{1,2,0:T(8,128)(2,1)} fusion(f32[4,512,1024]{1,2,0:T(8,128)} %get-tuple-element.29, f32[4,512]{1,0:T(4,128)S(1)} %get-tuple-element.28, bf16[2048,2,128]{2,0,1:T(8,128)(2,1)S(1)} %bitcast.160), kind=kOutput, calls=%fused_computation.52 | convolution fusion | flops 541327360 | bytes 9183232 | tf_op jit(solution)/shard_map/hqk,kd->qhd/dot_general | solution.py:32
  68.7 3.6 fusion.62
  72.2 3.8 fusion.33
  76.0 10.3 %fusion.59 = (f32[4,512]{1,0:T(4,128)S(1)}, f32[4,512,2048]{1,2,0:T(8,128)}) fusion(pred[512,2048]{0,1:T(8,128)(4,1)S(1)} %copy-done.4, bf16[512,4,128]{0,2,1:T(8,128)(2,1)} %bitcast.166, bf16[2048,2,128]{2,0,1:T(8,128)(2,1)S(1)} %bitcast.163), kind=kOutput, calls=%fused_computation.96 | convolution fusion | flops 1090521088 | bytes 18882560 | tf_op jit(solution)/shard_map/sub | solution.py:30
  86.3 8.4 %fusion.36 = bf16[4,512,128]{1,2,0:T(8,128)(2,1)S(1)} fusion(f32[4,512,2048]{1,2,0:T(8,128)} %get-tuple-element.25, f32[4,512]{1,0:T(4,128)S(1)} %get-tuple-element.24, bf16[2048,2,128]{2,0,1:T(8,128)(2,1)S(1)} %bitcast.164), kind=kOutput, calls=%fused_computation.54 | convolution fusion | flops 1082392576 | bytes 17833984 | tf_op jit(solution)/shard_map/hqk,kd->qhd/dot_general | solution.py:32
  94.8 4.4 convolution_convert_fusion.1
  99.9 77.7 %reduce-scatter.3.cloned.1.call-done = bf16[128,1024]{1,0:T(8,128)(2,1)} async-done(((bf16[2048,1024]{1,0:T(8,128)(2,1)}), bf16[128,1024]{1,0:T(8,128)(2,1)}) %reduce-scatter.3.cloned.1.call-update) | async-done | bytes 262160 | tf_op jit(solution)/shard_map/reduce_scatter | solution.py:61
  177.5 3.9 all-to-all-start.1
  182.0 66.6 %all-reduce = bf16[1024]{0:T(1024)(128)(2,1)S(1)} all-reduce(bf16[1024]{0:T(1024)(128)(2,1)S(1)} %dynamic-update-slice), channel_id=1, replica_groups=mesh['grp'=8,'tp'=16] {'grp','tp'}, use_global_device_ids=true, to_apply=%add | all-reduce | flops 1024 | bytes 4096
  249.2 69.1 %all-gather.3.cloned.1.call-done = bf16[128,28,1024]{2,1,0:T(8,128)(2,1)} async-done(((bf16[1,28,1024]{2,1,0:T(8,128)(2,1)}), bf16[128,28,1024]{2,1,0:T(8,128)(2,1)}) %all-gather.3.cloned.1.call-update) | async-done | bytes 7340048 | tf_op jit(solution)/shard_map/all_gather | solution.py:72
  318.3 10.9 %reshape.159 = bf16[3584,1024]{1,0:T(8,128)(2,1)} reshape(bf16[128,28,1024]{2,1,0:T(8,128)(2,1)} %all-gather.3.cloned.1.call-done) | data formatting | bytes 14680064
  329.2 4.9 convert_reduce_fusion
  334.1 7.3 %convolution_bitcast_fusion = f32[3584,1024]{0,1:T(8,128)} fusion(bf16[128,3584]{1,0:T(8,128)(2,1)S(1)} %copy-done.1, bf16[128,1024]{1,0:T(8,128)(2,1)S(1)} %get-tuple-element.32), kind=kOutput, calls=%fused_computation.13 | convolution fusion | flops 939524096 | bytes 15859712 | tf_op jit(solution)/shard_map/dot_general | solution.py:84
  341.5 63.6 %all-reduce.3 = (f32[]{:T(128)}, f32[1024]{0:T(1024)S(1)}) all-reduce(f32[]{:T(128)} %get-tuple-element.17, f32[1024]{0:T(1024)S(1)} %get-tuple-element.16), channel_id=1, replica_groups=mesh['grp'=8,'tp'=16] {'grp','tp'}, use_global_device_ids=true, to_apply=%region_10.11 | all-reduce | flops 1025 | bytes 8200 | tf_op jit(solution)/shard_map/psum | solution.py:80
  406.3 6.6 %convolution_convert_fusion = bf16[128,3584]{1,0:T(8,128)(2,1)} fusion(bf16[3584,1024]{1,0:T(8,128)(2,1)} %reshape.159, bf16[128,1024]{1,0:T(8,128)(2,1)S(1)} %get-tuple-element.32), kind=kOutput, calls=%fused_computation.26 | convolution fusion | flops 939982848 | bytes 8519680 | tf_op jit(solution)/shard_map/dot_general | solution.py:92
  412.9 100.5 %all-reduce.6.cloned.1.call-done = f32[3584,1024]{0,1:T(8,128)} async-done(((f32[3584,1024]{0,1:T(8,128)}), f32[3584,1024]{0,1:T(8,128)}) %all-reduce.6.cloned.1.call-update) | async-done | bytes 14680080
  513.3 1.4 constant_dynamic-slice_fusion
  (55 shorter events, 5.8 us)
Async XLA Ops:
  8.0 86.7 %copy-start = (bf16[512,1024]{1,0:T(8,128)(2,1)S(1)}, bf16[512,1024]{1,0:T(8,128)(2,1)}, u32[]{:S(2)}) copy-start(bf16[512,1024]{1,0:T(8,128)(2,1)} %param.10) | copy-start | bytes 3145732
  10.6 26.7 %all-to-all-start = ((bf16[128,2,16,128]{3,0,1,2:T(8,128)(2,1)}), bf16[128,2,16,128]{3,0,1,2:T(8,128)(2,1)S(1)}, u32[]{:S(2)}, u32[]{:S(2)}) async-start(bf16[128,2,16,128]{3,0,1,2:T(8,128)(2,1)} %bitcast.1), calls=%async_computation | async-start | bytes 2097152 | tf_op jit(solution)/shard_map/all_to_all | solution.py:55
  20.1 157.5 %reduce-scatter.3.cloned.1.call-start = ((), (), s32[]{:S(2)}) async-start(), calls=%async_computation.3 | async-start | bytes 4456448 | tf_op jit(solution)/shard_map/reduce_scatter | solution.py:61
  37.4 1.0 copy-start.2
  50.4 7.5 %copy-start.3 = (bf16[16,128,2,1,128]{4,1,0,2,3:T(8,128)(2,1)S(1)}, bf16[16,128,2,1,128]{4,1,0,2,3:T(8,128)(2,1)}, u32[]{:S(2)}) copy-start(bf16[16,128,2,1,128]{4,1,0,2,3:T(8,128)(2,1)} %copy-done.2) | copy-start | bytes 3145732
  50.4 7.5 %copy-start.6 = (pred[512,1024]{0,1:T(8,128)(4,1)S(1)}, pred[512,1024]{0,1:T(8,128)(4,1)}, u32[]{:S(2)}) copy-start(pred[512,1024]{0,1:T(8,128)(4,1)} %iota_compare_fusion.2) | copy-start | bytes 1572868
  50.4 7.5 %copy-start.7 = (bf16[1,512,512]{1,2,0:T(8,128)(2,1)S(1)}, bf16[1,512,512]{1,2,0:T(8,128)(2,1)}, u32[]{:S(2)}) copy-start(bf16[1,512,512]{1,2,0:T(8,128)(2,1)} %copy.78) | copy-start | bytes 1572868
  63.0 5.6 %copy-start.5 = (bf16[1,512,512]{1,2,0:T(8,128)(2,1)S(1)}, bf16[1,512,512]{1,2,0:T(8,128)(2,1)}, u32[]{:S(2)}) copy-start(bf16[1,512,512]{1,2,0:T(8,128)(2,1)} %copy.77) | copy-start | bytes 1572868
  72.2 3.8 copy-start.4
  86.3 8.4 %copy-start.11 = (bf16[4,512,128]{1,2,0:T(8,128)(2,1)S(1)}, bf16[4,512,128]{1,2,0:T(8,128)(2,1)}, u32[]{:S(2)}) copy-start(bf16[4,512,128]{1,2,0:T(8,128)(2,1)} %fusion.35) | copy-start | bytes 1572868
  86.3 8.4 %copy-start.12 = (bf16[4,512,128]{1,2,0:T(8,128)(2,1)S(1)}, bf16[4,512,128]{1,2,0:T(8,128)(2,1)}, u32[]{:S(2)}) copy-start(bf16[4,512,128]{1,2,0:T(8,128)(2,1)} %fusion.34) | copy-start | bytes 1572868
  86.3 8.4 %copy-start.13 = (bf16[4,512,128]{1,2,0:T(8,128)(2,1)S(1)}, bf16[4,512,128]{1,2,0:T(8,128)(2,1)}, u32[]{:S(2)}) copy-start(bf16[4,512,128]{1,2,0:T(8,128)(2,1)} %fusion.33) | copy-start | bytes 1572868
  94.8 5.0 copy-start.8
  94.8 86.9 %copy-start.9 = (bf16[8]{0:T(256)(128)(2,1)S(1)}, bf16[8]{0:T(256)(128)(2,1)}, u32[]{:S(2)}) copy-start(bf16[8]{0:T(256)(128)(2,1)} %param.15) | copy-start | bytes 52
  94.8 153.7 %copy-start.10 = (s32[128]{0:T(128)S(1)}, s32[128]{0:T(128)}, u32[]{:S(2)}) copy-start(s32[128]{0:T(128)} %param.12) | copy-start | bytes 1540
  99.2 219.0 %all-gather.3.cloned.1.call-start = ((), (), s32[]{:S(2)}) async-start(), calls=%async_computation.4 | async-start | bytes 8454144 | tf_op jit(solution)/shard_map/all_gather | solution.py:72
  177.5 71.0 %all-to-all-start.1 = ((bf16[8,16,1024]{2,1,0:T(8,128)(2,1)}), bf16[8,16,1024]{2,1,0:T(8,128)(2,1)S(1)}, u32[]{:S(2)}, u32[]{:S(2)}) async-start(bf16[8,16,1024]{2,1,0:T(8,128)(2,1)} %bitcast.169), calls=%async_computation.2 | async-start | bytes 524288 | tf_op jit(solution)/shard_map/all_to_all | solution.py:69
  181.5 331.8 %all-reduce.6.cloned.1.call-start = ((), (), s32[]{:S(2)}) async-start(), calls=%async_computation.5 | async-start | bytes 29360128
  248.5 80.7 %copy-start.1 = (bf16[128,3584]{1,0:T(8,128)(2,1)S(1)}, bf16[128,3584]{1,0:T(8,128)(2,1)}, u32[]{:S(2)}) copy-start(bf16[128,3584]{1,0:T(8,128)(2,1)} %param.13) | copy-start | bytes 2752516
Sparse Core Ops, SparseCore 0:
  99.4 78.1 reduce-scatter.2
Sparse Core Ops, SparseCore 1:
  101.6 216.7 all-gather.2
  341.5 171.7 all-reduce.5
where the time goes:
time: 525 us; the launch traced here: 524 us
  waiting for transfers between devices  250 us (48%)
  blocking collectives  130 us (25%)
  matrix products  69.2 us (13%)
  local copies, waits for them, and re-layouts  28.8 us (5%)
  between operations  17.5 us (3%)
  other arithmetic  15 us (3%)
  starting transfers between devices  13.5 us (3%)
    unnamed x4, waiting for transfers between devices  101 us
    reduce_scatter x1, waiting for transfers between devices, on_device(): lax.psum_scatter(jnp.dot(attention, projector, preferred_element_type=jnp...  77.7 us
    all_gather x1, waiting for transfers between devices, on_device(): lax.all_gather(student_weight, ('grp', 'tp'), axis=0, tiled=True)  69.1 us
    unnamed x1, blocking collectives  66.6 us
    psum x1, blocking collectives, on_device(): loss_sum = lax.psum(jnp.sum(residual * residual), ('grp', 'tp'))  63.6 us
    dot_general x4, matrix products, attend(): jnp.einsum('hqk,kd->qhd', prob_rows, value_rows[:last_row], preferred_ele...  25.3 us
    unnamed x39, local copies, waits for them, and re-layouts  23.7 us
    sub x3, matrix products, attend(): weights = jnp.exp(scores - row_peak)  19 us
  transfers between devices with their start and end apart: 5, of which 4 were waited for; matrix products, arithmetic and copies ran while one was open for 4% of the time, Pallas kernels for 0%

commit v1 on v0

v1 whole, which is shorter than its diff:
```python
import functools

import jax
import jax.numpy as jnp
from jax import lax
from jax.experimental import pallas as pl
from jax.experimental.pallas import tpu as pltpu
from jax.sharding import PartitionSpec as P

MESH = pl.DeviceIdType.MESH
TEXT_IDS = 151643
SCALE = 128 ** -0.5 * 1.4426950408889634
BF = jnp.bfloat16
F32 = jnp.float32


def rcopy(src, dst, send_sem, recv_sem, grp, tp):
    return pltpu.make_async_remote_copy(
        src_ref=src, dst_ref=dst, send_sem=send_sem, recv_sem=recv_sem,
        device_id=(grp, tp), device_id_type=MESH)


def loop(first, last, body):
    lax.fori_loop(first, last, lambda i, carry: (body(i), carry)[1], 0)


def attend(core, c, qo, qs, keys, values, S, mx, acc, out):
    T = 256

    def score(j, masked):
        at = pl.ds(pl.multiple_of(j * T, T), T)
        kt = keys[at, :]
        if masked:
            row = lax.broadcasted_iota(jnp.int32, (128, T), 0) + core * 128
            keep = row >= lax.broadcasted_iota(jnp.int32, (128, T), 1)
        for h in range(8):
            hr = slice(h * 128, (h + 1) * 128)
            q = (qo if h < 4 else qs)[:, (h % 4) * 128:(h % 4) * 128 + 128]
            s = lax.dot_general(q, kt, (((1,), (1,)), ((), ())), preferred_element_type=F32)
            if masked:
                s = jnp.where(keep, s, -1e30)
            S[hr, at] = s
            m = jnp.maximum(mx[hr, :], jnp.maximum(s[:, :128], s[:, 128:]))
            if masked:
                m = jnp.broadcast_to(jnp.max(m, axis=1, keepdims=True) * SCALE, (128, 128))
            mx[hr, :] = m

    mx[...] = jnp.full_like(mx, -1e30)
    loop(0, c, lambda j: score(j, False))
    score(c, True)
    acc[...] = jnp.zeros_like(acc)

    def weigh(off, W):
        vt = values[pl.ds(off, W), :]
        vt = jnp.concatenate([vt, jnp.ones_like(vt)], axis=1)
        for h in range(8):
            hr = slice(h * 128, (h + 1) * 128)
            m = mx[hr, :]
            ps = []
            for w in range(W // 128):
                s = S[hr, pl.ds(pl.multiple_of(off + w * 128, 128), 128)]
                ps.append(jnp.exp2(s * SCALE - m).astype(BF))
            acc[hr, :] += jnp.dot(jnp.concatenate(ps, axis=1), vt, preferred_element_type=F32)

    n = c + 1
    loop(0, n // 2, lambda j: weigh(pl.multiple_of(j * 512, 512), 512))
    loop(0, n % 2, lambda j: weigh(pl.multiple_of((n - 1) * 256, 256), 256))
    for h in range(8):
        a = acc[h * 128:(h + 1) * 128, :]
        out[:, h * 128:(h + 1) * 128] = (a[:, :128] / a[:, 128:]).astype(BF)


def kernel(q_in, kv_in, proj_in, own_in, ids_in, x_in, w_in,
           wg_out, small_out, ig_out,
           qo, qs, keys, values, S, mx, acc, att, proj_o, proj_s, tsend, tland, tsum, pland,
           xland, xt, wland, wz, brow, osend, oland, eland, wg, wsend, wgland, igsend, igland,
           l_sem, qp_s, qp_r, k_s, k_r, v_s, v_r, rk_s, rv_s, w_s, w_r, x_s, x_r, o_s, o_r,
           t_s, t_r, p_s, p_r, e_s, e_r, re_s, g_s, g_r, i_s, i_r):
    g = lax.axis_index("grp")
    t = lax.axis_index("tp")
    x, yl = lax.rem(g, 4), g // 4
    core, chip = lax.rem(t, 2), t // 2
    sib = chip * 2 + 1 - core
    m = core * 4 + x
    src16 = chip * 2 + yl

    def member(i):
        return yl * 4 + lax.rem(i, 4), chip * 2 + i // 4

    def plane(i):
        return lax.rem(i, 2) * 4 + x, (i // 2) * 2 + yl

    own_kv = pl.ds(pl.multiple_of(t * 128, 128), 128)
    kcol = pl.ds(pl.multiple_of(chip * 128, 128), 128)
    vcol = pl.ds(pl.multiple_of(1024 + chip * 128, 128), 128)

    def window(i):
        return pl.ds(pl.multiple_of((i // 2) * 896 + lax.rem(i, 2) * 384, 128), 512)

    local = [
        pltpu.make_async_copy(kv_in.at[:, kcol], keys.at[own_kv, :], l_sem.at[0]),
        pltpu.make_async_copy(kv_in.at[:, vcol], values.at[own_kv, :], l_sem.at[1]),
        pltpu.make_async_copy(q_in.at[:, core], qo, l_sem.at[2]),
        pltpu.make_async_copy(proj_in, proj_o, l_sem.at[3]),
        pltpu.make_async_copy(x_in.at[:, window(m)], xland.at[m], l_sem.at[4]),
    ]
    for copy in local:
        copy.start()

    barrier = pltpu.get_barrier_semaphore()

    def greet(grp, tp):
        pl.semaphore_signal(barrier, inc=1, device_id=(grp, tp), device_id_type=MESH)

    def greet_plane(i):
        j = lax.rem(yl * 16 + t + i, 32)
        greet((j // 16) * 4 + x, lax.rem(j, 16))

    loop(1, 32, greet_plane)

    def greet_x(i):
        xx = lax.rem(x + i, 4)
        greet(yl * 4 + xx, t)
        greet(yl * 4 + xx, sib)
        greet((1 - yl) * 4 + xx, t)

    loop(1, 4, greet_x)
    pl.semaphore_wait(barrier, 31 + 9)

    def kv_cols(q):
        return (pl.ds(pl.multiple_of(q * 128, 128), 128),
                pl.ds(pl.multiple_of(1024 + q * 128, 128), 128))

    def kv_send(i, start):
        q = lax.rem(chip + i, 8)
        kc, vc = kv_cols(q)
        a = rcopy(kv_in.at[:, kc], keys.at[own_kv, :], k_s.at[q], k_r.at[t], g, q * 2 + core)
        b = rcopy(kv_in.at[:, vc], values.at[own_kv, :], v_s.at[q], v_r.at[t], g, q * 2 + core)
        if start:
            a.start()
            b.start()
        else:
            a.wait_send()
            b.wait_send()

    loop(1, 8, lambda i: kv_send(i, True))
    qcopy = rcopy(q_in.at[:, 1 - core], qs, qp_s.at[0], qp_r.at[0], g, sib)
    pcopy = rcopy(proj_in, proj_s, qp_s.at[1], qp_r.at[1], g, sib)
    qcopy.start()

    def kv_relay(src, start):
        rows = pl.ds(pl.multiple_of(src * 128, 128), 128)
        a = rcopy(keys.at[rows, :], keys.at[rows, :], rk_s.at[src // 2], k_r.at[src], g, sib)
        b = rcopy(values.at[rows, :], values.at[rows, :], rv_s.at[src // 2], v_r.at[src], g, sib)
        if start:
            a.start()
            b.start()
        else:
            a.wait_send()
            b.wait_send()

    def kv_wait(src):
        rows = pl.ds(pl.multiple_of(src * 128, 128), 128)
        rcopy(keys.at[rows, :], keys.at[rows, :], k_s.at[0], k_r.at[src], g, sib).wait_recv()
        rcopy(values.at[rows, :], values.at[rows, :], v_s.at[0], v_r.at[src], g, sib).wait_recv()

    local[0].wait()
    local[1].wait()
    kv_relay(t, True)

    def w_send(i, start):
        i = lax.rem(src16 + i, 16)
        dg, dt = plane(i)
        here = (i == src16) & (core == yl)

        if start:
            @pl.when(here)
            def _():
                pltpu.make_async_copy(w_in, wland.at[t], w_r.at[t]).start()

        @pl.when(jnp.logical_not(here))
        def _():
            copy = rcopy(w_in, wland.at[t], w_s.at[i], w_r.at[t], dg, dt)
            if start:
                copy.start()
            else:
                copy.wait_send()

    def x_send(i, start):
        j = lax.rem(m + i, 8)
        dg, dt = member(j)
        copy = rcopy(x_in.at[:, window(j)], xland.at[m], x_s.at[j], x_r.at[m], dg, dt)
        if start:
            copy.start()
        else:
            copy.wait_send()

    def kv_pass(i):
        src = lax.rem(chip + 8 - i, 8) * 2 + core
        kv_wait(src)
        kv_relay(src, True)

    loop(1, 8, kv_pass)
    pcopy.start()
    loop(0, 16, lambda i: w_send(i, True))
    loop(1, 8, lambda i: x_send(i, True))

    loop(0, 8, lambda i: kv_wait(i * 2 + 1 - core))
    local[2].wait()
    qcopy.wait_recv()

    def t_send(q, start):
        copy = rcopy(tsend.at[q], tland.at[chip], t_s.at[q], t_r.at[chip], g, q * 2 + core)
        if start:
            copy.start()
        else:
            copy.wait_send()

    def o_send(i, start):
        j = lax.rem(m + i, 8)
        dg, dt = member(j)
        copy = rcopy(osend.at[j], oland.at[m], o_s.at[j], o_r.at[m], dg, dt)
        if start:
            copy.start()
        else:
            copy.wait_send()

    off = pl.multiple_of(lax.rem(x, 2) * 64, 64)

    def student_forward():
        loop(0, 16, lambda i: pltpu.make_async_copy(w_in, wland.at[i], w_r.at[i]).wait())
        wz[...] = jnp.zeros_like(wz)
        bias = jnp.zeros((1, 1024), F32)
        for a in range(4):
            rows = [wland[4 * a + b].astype(F32) for b in range(4)]
            for r in rows:
                bias = bias + r[28:29]
            wz[pl.ds(off + a * 112, 112), :] = jnp.concatenate([r[:28] for r in rows], axis=0).astype(BF)
        brow[...] = bias
        local[4].wait()

        def one(i):
            j = lax.rem(m + i, 8)

            @pl.when(i > 0)
            def _():
                rcopy(xland.at[j], xland.at[j], x_s.at[0], x_r.at[j], g, sib).wait_recv()

            xw = xland[j]
            xt[j] = jnp.transpose(xw)
            for n in range(4):
                cols = slice(n * 256, (n + 1) * 256)
                o = jnp.dot(xw, wz[:, cols], preferred_element_type=F32) + brow[:, cols]
                osend[j, :, cols] = o.astype(BF)

            @pl.when(i > 0)
            def _():
                o_send(i, True)

        loop(0, 8, one)
        oland[m] = osend[m]

    local[3].wait()
    pcopy.wait_recv()

    def chunk(i):
        c = lax.rem(chip + 1 + i, 8)

        @pl.when(i == 3)
        def _():
            student_forward()

        attend(core, c, qo.at[c], qs.at[c], keys, values, S, mx, acc, att)
        for n in range(4):
            cols = slice(n * 256, (n + 1) * 256)
            p = jnp.dot(att[:, :512], proj_o[:, cols], preferred_element_type=F32)
            p = p + jnp.dot(att[:, 512:], proj_s[:, cols], preferred_element_type=F32)
            tsend[c, :, cols] = p.astype(BF)

        @pl.when(i < 7)
        def _():
            t_send(c, True)

    loop(0, 8, chunk)
    tland[chip] = tsend[chip]

    def t_wait(i):
        q = lax.rem(chip + i, 8)
        rcopy(tland.at[q], tland.at[q], t_s.at[0], t_r.at[q], g, sib).wait_recv()

    loop(1, 8, t_wait)
    for n in range(4):
        cols = slice(n * 256, (n + 1) * 256)
        total = tland[0, :, cols].astype(F32)
        for q in range(1, 8):
            total = total + tland[q, :, cols].astype(F32)
        tsum[:, :, cols] = total.astype(BF).reshape(8, 16, 256)

    def p_send(i, start):
        j = lax.rem(g + i, 8)
        copy = rcopy(tsum.at[j], pland.at[g], p_s.at[j], p_r.at[g], j, t)
        if start:
            copy.start()
        else:
            copy.wait_send()

    loop(1, 8, lambda i: p_send(i, True))
    pland[g] = tsum[g]

    def o_wait(i):
        j = lax.rem(m + i, 8)
        rcopy(oland.at[j], oland.at[j], o_s.at[0], o_r.at[j], g, sib).wait_recv()

    loop(1, 8, o_wait)

    def p_wait(i):
        j = lax.rem(g + i, 8)
        rcopy(pland.at[j], pland.at[j], p_s.at[0], p_r.at[j], g, sib).wait_recv()

    loop(1, 8, p_wait)
    keep = jnp.where(ids_in[...] < TEXT_IDS, 1.0, 0.0).astype(F32)
    keep = jnp.transpose(jnp.broadcast_to(keep, (128, 128)))
    for k in range(8):
        rows = slice(k * 16, (k + 1) * 16)
        o = oland[0, rows, :].astype(F32)
        for j in range(1, 8):
            o = o + oland[j, rows, :].astype(F32)
        paired = pland[own_in[k]].astype(F32)
        kk = jnp.concatenate([keep[rows]] * 8, axis=1)
        eland[m, rows, :] = (kk * (o - paired)).astype(BF)

    def e_send(i, start):
        xx = lax.rem(x + i, 4)
        copy = rcopy(eland.at[m], eland.at[m], e_s.at[i], e_r.at[m], yl * 4 + xx, t)
        if start:
            copy.start()
        else:
            copy.wait_send()

    def e_relay(i, start):
        j = core * 4 + lax.rem(x + i, 4)
        copy = rcopy(eland.at[j], eland.at[j], re_s.at[i], e_r.at[j], g, sib)
        if start:
            copy.start()
        else:
            copy.wait_send()

    def e_wait(j):
        rcopy(eland.at[j], eland.at[j], e_s.at[0], e_r.at[j], g, sib).wait_recv()

    loop(1, 4, lambda i: e_send(i, True))
    e_relay(0, True)

    def e_pass(i):
        e_wait(core * 4 + lax.rem(x + i, 4))
        e_relay(i, True)

    loop(1, 4, e_pass)
    loop(0, 4, lambda i: e_wait((1 - core) * 4 + i))

    def i_send(i, start):
        j = lax.rem(m + i, 8)
        dg, dt = member(j)
        copy = rcopy(igsend.at[j], igland.at[m], i_s.at[j], i_r.at[m], dg, dt)
        if start:
            copy.start()
        else:
            copy.wait_send()

    def input_grad(i):
        j = lax.rem(m + i, 8)
        igsend[j] = lax.dot_general(eland[j], wz[...], (((1,), (1,)), ((), ())),
                                    preferred_element_type=F32).astype(BF)

        @pl.when(i < 8)
        def _():
            i_send(i, True)

    esum = []
    lsum = []
    for n in range(4):
        cols = slice(n * 256, (n + 1) * 256)
        total = jnp.zeros((512, 256), F32)
        eb = jnp.zeros((8, 256), F32)
        lb = jnp.zeros((8, 256), F32)
        for j in range(8):
            e = eland[j, :, cols]
            total = total + jnp.dot(xt[j], e, preferred_element_type=F32)
            ef = e.astype(F32)
            for r in range(16):
                er = ef[r * 8:(r + 1) * 8]
                eb = eb + er
                lb = lb + er * er
        wg[:, cols] = total
        esum.append(jnp.sum(eb, axis=0, keepdims=True))
        lsum.append(jnp.sum(lb, axis=0, keepdims=True))
    esum = jnp.concatenate(esum, axis=1)
    lsum = jnp.concatenate(lsum, axis=1)
    ehi = esum.astype(BF).astype(F32)
    lhi = lsum.astype(BF).astype(F32)
    extra = [ehi, esum - ehi, lhi, lsum - lhi]

    def g_send(i, start):
        here = (c_is_yl) & (i == t)

        if start:
            @pl.when(here)
            def _():
                pltpu.make_async_copy(wsend.at[i], wgland.at[src16], g_r.at[src16]).start()

        @pl.when(jnp.logical_not(here))
        def _():
            copy = rcopy(wsend.at[i], wgland.at[src16], g_s.at[i], g_r.at[src16], core * 4 + x, i)
            if start:
                copy.start()
            else:
                copy.wait_send()

    c_is_yl = core == yl
    row = lax.broadcasted_iota(jnp.int32, (32, 1024), 0)
    for i in range(16):
        v = wg[pl.ds(off + (28 * i) // 8 * 8, 32), :]
        if (28 * i) % 8:
            v = pltpu.roll(v, 28, 0)
        for r in range(4):
            v = jnp.where(row == 28 + r, extra[r], v)
        wsend[i] = v.astype(BF)
    loop(0, 16, lambda i: g_send(lax.rem(t + i, 16), True))
    loop(1, 9, input_grad)
    igland[m] = igsend[m]

    loop(0, 16, lambda i: pltpu.make_async_copy(wsend.at[i], wgland.at[i], g_r.at[i]).wait())
    total = wgland[0].astype(F32)
    for i in range(1, 16):
        total = total + wgland[i].astype(F32)
    wg_out[...] = total[:28]
    small_out[...] = total[24:32]

    def i_wait(i):
        j = lax.rem(m + i, 8)
        rcopy(igland.at[j], igland.at[j], i_s.at[0], i_r.at[j], g, sib).wait_recv()

    loop(1, 8, i_wait)
    for b in range(4):
        ig_out[:, b * 896:b * 896 + 384] = igland[2 * b, :, :384]
        ig_out[:, b * 896 + 384:b * 896 + 512] = igland[2 * b, :, 384:] + igland[2 * b + 1, :, :128]
        ig_out[:, b * 896 + 512:(b + 1) * 896] = igland[2 * b + 1, :, 128:]

    loop(1, 8, lambda i: kv_send(i, False))
    qcopy.wait_send()
    pcopy.wait_send()
    loop(0, 8, lambda i: kv_relay(i * 2 + core, False))
    loop(0, 16, lambda i: w_send(i, False))
    loop(1, 8, lambda i: x_send(i, False))
    loop(1, 8, lambda i: o_send(i, False))
    loop(1, 8, lambda i: t_send(lax.rem(chip + i, 8), False))
    loop(1, 8, lambda i: p_send(i, False))
    loop(1, 4, lambda i: e_send(i, False))
    loop(0, 4, lambda i: e_relay(i, False))
    loop(0, 16, lambda i: g_send(i, False))
    loop(1, 8, lambda i: i_send(i, False))


def on_device(queries, keys_values, projector, ownership, token_ids, student_input, student_weight, student_bias):
    d = lax.axis_index("grp") * 16 + lax.axis_index("tp")
    bias_row = lax.dynamic_update_slice(jnp.zeros((4, 1024), BF), student_bias[None], (0, d * 8))
    w_pad = jnp.concatenate([student_weight, bias_row], axis=0)
    hbm = pl.BlockSpec(memory_space=pl.ANY)
    vmem = pl.BlockSpec(memory_space=pltpu.VMEM)
    smem = pl.BlockSpec(memory_space=pltpu.SMEM)
    dma = pltpu.SemaphoreType.DMA
    V = pltpu.VMEM
    wg, small, ig = pl.pallas_call(
        kernel,
        out_shape=(jax.ShapeDtypeStruct((28, 1024), F32), jax.ShapeDtypeStruct((8, 1024), F32),
                   jax.ShapeDtypeStruct((128, 3584), BF)),
        in_specs=[hbm, hbm, hbm, smem, vmem, hbm, hbm],
        out_specs=(vmem, vmem, vmem),
        scratch_shapes=[
            V((8, 128, 512), BF), V((8, 128, 512), BF), V((2048, 128), BF), V((2048, 128), BF),
            V((1024, 2048), F32), V((1024, 128), F32), V((1024, 256), F32), V((128, 1024), BF),
            V((512, 1024), BF), V((512, 1024), BF), V((8, 128, 1024), BF), V((8, 128, 1024), BF),
            V((8, 16, 1024), BF), V((8, 16, 1024), BF),
            V((8, 128, 512), BF), V((8, 512, 128), BF), V((16, 32, 1024), BF), V((512, 1024), BF), V((1, 1024), F32),
            V((8, 128, 1024), BF), V((8, 128, 1024), BF), V((8, 128, 1024), BF),
            V((512, 1024), F32), V((16, 32, 1024), BF), V((16, 32, 1024), BF),
            V((8, 128, 512), BF), V((8, 128, 512), BF),
            dma((5,)), dma((2,)), dma((2,)), dma((8,)), dma((16,)), dma((8,)), dma((16,)), dma((8,)), dma((8,)),
            dma((16,)), dma((16,)), dma((8,)), dma((8,)), dma((8,)), dma((8,)),
            dma((8,)), dma((8,)), dma((8,)), dma((8,)), dma((4,)), dma((8,)), dma((4,)), dma((16,)), dma((16,)),
            dma((8,)), dma((8,)),
        ],
        compiler_params=pltpu.CompilerParams(
            collective_id=0, has_side_effects=True, vmem_limit_bytes=60 * 2 ** 20),
        cost_estimate=pl.CostEstimate(flops=9 * 10 ** 9, bytes_accessed=8 * 10 ** 6, transcendentals=9 * 10 ** 6),
    )(queries.reshape(8, 2, 128, 512), keys_values[0], projector, ownership, token_ids.reshape(1, 128),
      student_input, w_pad)
    loss = (jnp.sum(small[6]) + jnp.sum(small[7])) / 32768.0
    bias = lax.dynamic_slice(small[4] + small[5], (d * 8,), (8,))
    return loss, wg, bias, ig


def solution(mesh):
    return jax.shard_map(
        on_device,
        mesh=mesh,
        in_specs=(
            P("grp", None, "tp"), P("grp", "tp", None), P("tp", None), P(), P(("grp", "tp")),
            P(("grp", "tp"), None), P(("grp", "tp"), None), P(("grp", "tp")),
        ),
        out_specs=(P(), P(("grp", "tp"), None), P(("grp", "tp")), P(("grp", "tp"), None)),
        check_vma=False,
    )
```

time: 525 us -> 124 us (0.24)
  waiting for transfers between devices: 250 us -> 0 us
  blocking collectives: 130 us -> 0 us
  Pallas kernels: 0 us -> 111 us
  matrix products: 69.2 us -> 0 us
  local copies, waits for them, and re-layouts: 28.8 us -> 4.64 us
  between operations: 17.5 us -> 3.09 us
  starting transfers between devices: 13.5 us -> 0 us
  other arithmetic: 15 us -> 3.6 us
    pallas_call x0 -> x1, Pallas kernels: none -> 111 us  [on_device(): pl.pallas_call(kernel, out_shape=(jax.ShapeDtypeStruct((28, 1024), F32),...]
    unnamed x4 -> x0, waiting for transfers between devices: 101 us -> none
    reduce_scatter x1 -> x0, waiting for transfers between devices: 77.7 us -> none  [on_device(): lax.psum_scatter(jnp.dot(attention, projector, preferred_element_type=jnp...]
    all_gather x1 -> x0, waiting for transfers between devices: 69.1 us -> none  [on_device(): lax.all_gather(student_weight, ('grp', 'tp'), axis=0, tiled=True)]
    unnamed x1 -> x0, blocking collectives: 66.6 us -> none
    psum x1 -> x0, blocking collectives: 63.6 us -> none  [on_device(): loss_sum = lax.psum(jnp.sum(residual * residual), ('grp', 'tp'))]
    dot_general x9 -> x0, matrix products: 50.2 us -> none  [the longest x4 25.3 us: attend(): jnp.einsum('hqk,kd->qhd', prob_rows, value_rows[:last_row], preferred_ele...]
    unnamed x39 -> x2, local copies, waits for them, and re-layouts: 23.7 us -> 3.73 us
  transfers between devices with their start and end apart: 5 -> 0, of which waited for: 4 -> 0; matrix products, arithmetic and copies ran while one was open for 4% -> 0% of each run, Pallas kernels for 0% -> 0%
where the time goes in v1:
time: 124 us; the launch traced here: 122 us
  Pallas kernels  111 us (90%)
  local copies, waits for them, and re-layouts  4.64 us (4%)
  other arithmetic  3.6 us (3%)
  between operations  3.09 us (2%)
    pallas_call x1, Pallas kernels, on_device(): pl.pallas_call(kernel, out_shape=(jax.ShapeDtypeStruct((28, 1024), F32),...  111 us
    unnamed x2, local copies, waits for them, and re-layouts  3.73 us

profile of v1, /device:TPU:1, one launch (start us, length us, event | category | flops | bytes accessed | tf_op | source)
XLA Modules:
  0.0 122.5 jit_solution(2203692914368050402)
XLA Ops:
  0.6 0.9 dynamic_update_slice.3
  1.6 1.5 %pad_maximum_fusion.w_in = bf16[32,1024]{1,0:T(8,128)(2,1)} fusion(bf16[4,1024]{1,0:T(4,128)(2,1)S(1)} %dynamic_update_slice.3, bf16[28,1024]{1,0:T(8,128)(2,1)} %param.14), kind=kLoop, calls=%fused_computation | loop fusion | flops 131072 | bytes 131072 | tf_op jit(solution)/shard_map/concatenate | solution.py:467
  3.0 111.1 %shard_map.111 = (f32[28,1024]{1,0:T(8,128)}, f32[8,1024]{1,0:T(8,128)}, bf16[128,3584]{1,0:T(8,128)(2,1)}) custom-call(bf16[8,2,128,512]{3,2,1,0:T(8,128)(2,1)} %bitcast.7, bf16[128,2048]{1,0:T(8,128)(2,1)} %bitcast.8, bf16[512,1024]{1,0:T(8,128)(2,1)} %proj_in.1, s32[8]{0:T(128)} %own_in.1, s32[1,128]{1,0:T(1,128)} %bitcast.9, bf16[128,3584]{1,0:T(8,128)(2,1)} %x_in.1, ...), custom_call_target="tpu_custom_call" | custom-call | flops 8999999488 | bytes 8000000 | tf_op jit(solution)/shard_map/pallas_call | solution.py:473
  114.2 1.5 %slice_reduce_fusion = (f32[]{:T(128)}, f32[]{:T(128)}, f32[1,1024]{1,0:T(1,128)S(1)}, f32[1,1024]{1,0:T(1,128)S(1)}) fusion(f32[8,1024]{1,0:T(8,128)} %get-tuple-element.7), kind=kLoop, calls=%fused_computation.1 | loop fusion | flops 2046 | bytes 24584 | tf_op jit(solution)/shard_map/reduce_sum | solution.py:498
  117.0 0.6 fusion
  117.6 1.6 %copy.15 = f32[28,1024]{1,0:T(8,128)} copy(f32[28,1024]{1,0:T(8,128)} %get-tuple-element.19) | data formatting | bytes 229376
  119.2 2.2 %copy.16 = bf16[128,3584]{1,0:T(8,128)(2,1)} copy(bf16[128,3584]{1,0:T(8,128)(2,1)} %get-tuple-element.21) | data formatting | bytes 1835008
  (1 shorter events, 0.0 us)

commit v2 on v1

--- a/solution.py
+++ b/solution.py
@@ -70,12 +70,12 @@
         out[:, h * 128:(h + 1) * 128] = (a[:, :128] / a[:, 128:]).astype(BF)
 
 
-def kernel(q_in, kv_in, proj_in, own_in, ids_in, x_in, w_in,
-           wg_out, small_out, ig_out,
-           qo, qs, keys, values, S, mx, acc, att, proj_o, proj_s, tsend, tland, tsum, pland,
-           xland, xt, wland, wz, brow, osend, oland, eland, wg, wsend, wgland, igsend, igland,
-           l_sem, qp_s, qp_r, k_s, k_r, v_s, v_r, rk_s, rv_s, w_s, w_r, x_s, x_r, o_s, o_r,
-           t_s, t_r, p_s, p_r, e_s, e_r, re_s, g_s, g_r, i_s, i_r):
+def kernel(q_in, kv_in, proj_in, own_in, ids_in, x_in, w_in, b_in,
+           wgland, igland,
+           qo, qs, keys, values, S, mx, acc, att, proj_o, proj_s, tsend, ta, ta2, tb, tbsum, tb2, tsum, pland,
+           xland, xt, w_pad, wland, wz, brow, osib, oswap, osend, oland, eland, wg, wsend, igsend,
+           l_sem, qp_s, qp_r, k_s, k_r, v_s, v_r, rk_s, rv_s, w_s, w_r, x_s, x_r, os_s, os_r, o_s, o_r,
+           ta_s, ta_r, tb_s, tb_r, ta2_s, ta2_r, tb2_s, tb2_r, p_s, p_r, e_s, e_r, re_s, g_s, g_r, i_s, i_r):
     g = lax.axis_index("grp")
     t = lax.axis_index("tp")
     x, yl = lax.rem(g, 4), g // 4
@@ -107,6 +107,13 @@
     for copy in local:
         copy.start()
 
+    lane = lax.broadcasted_iota(jnp.int32, (4, 1024), 1) - (g * 16 + t) * 8
+    first = lax.broadcasted_iota(jnp.int32, (4, 1024), 0) == 0
+    b_row = jnp.zeros((4, 1024), F32)
+    for r in range(8):
+        b_row = jnp.where(first & (lane == r), jnp.broadcast_to(b_in[:, r:r + 1].astype(F32), (4, 1024)), b_row)
+    w_pad[...] = jnp.concatenate([w_in[...].astype(F32), b_row], axis=0).astype(BF)
+
     barrier = pltpu.get_barrier_semaphore()
 
     def greet(grp, tp):
@@ -176,11 +183,11 @@
         if start:
             @pl.when(here)
             def _():
-                pltpu.make_async_copy(w_in, wland.at[t], w_r.at[t]).start()
+                pltpu.make_async_copy(w_pad, wland.at[t], w_r.at[t]).start()
 
         @pl.when(jnp.logical_not(here))
         def _():
-            copy = rcopy(w_in, wland.at[t], w_s.at[i], w_r.at[t], dg, dt)
+            copy = rcopy(w_pad, wland.at[t], w_s.at[i], w_r.at[t], dg, dt)
             if start:
                 copy.start()
             else:
@@ -209,17 +216,48 @@
     local[2].wait()
     qcopy.wait_recv()
 
-    def t_send(q, start):
-        copy = rcopy(tsend.at[q], tland.at[chip], t_s.at[q], t_r.at[chip], g, q * 2 + core)
+    cz, ch = chip // 2, lax.rem(chip, 2)
+    A, B = pl.ds(0, 512), pl.ds(512, 512)
+
+    def ta_send(c, start):
+        copy = rcopy(tsend.at[c, :, A], ta.at[lax.rem(c, 2), cz], ta_s.at[c], ta_r.at[lax.rem(c, 2) * 4 + cz],
+                     g, (c // 2 * 2 + ch) * 2 + core)
+        if start:
+            copy.start()
+        else:
+            copy.wait_send()
+
+    def ta_wait(h, z):
+        rcopy(ta.at[h, z], ta.at[h, z], ta_s.at[0], ta_r.at[h * 4 + z], g, sib).wait_recv()
+
+    def ta2_send():
+        return rcopy(ta2.at[0], ta2.at[1], ta2_s.at[0], ta2_r.at[0], g, (cz * 2 + 1 - ch) * 2 + core)
+
+    def tb_send(z, start):
+        copy = rcopy(tsend.at[z * 2 + 1 - ch, :, B], tb.at[z], tb_s.at[z], tb_r.at[z],
+                     g, (cz * 2 + 1 - ch) * 2 + core)
+        if start:
+            copy.start()
+        else:
+            copy.wait_send()
+
+    def tb2_send(z, start):
+        copy = rcopy(tbsum.at[z], tb2.at[cz], tb2_s.at[z], tb2_r.at[cz], g, (z * 2 + ch) * 2 + core)
+        if start:
+            copy.start()
+        else:
+            copy.wait_send()
+
+    def os_send(i, start):
+        copy = rcopy(osib.at[i], oswap.at[i], os_s.at[i], os_r.at[i], g, sib)
         if start:
             copy.start()
         else:
             copy.wait_send()
 
     def o_send(i, start):
-        j = lax.rem(m + i, 8)
-        dg, dt = member(j)
-        copy = rcopy(osend.at[j], oland.at[m], o_s.at[j], o_r.at[m], dg, dt)
+        xx = lax.rem(x + i, 4)
+        copy = rcopy(osend.at[xx], oland.at[x], o_s.at[xx], o_r.at[x], yl * 4 + xx, t)
         if start:
             copy.start()
         else:
@@ -228,7 +266,7 @@
     off = pl.multiple_of(lax.rem(x, 2) * 64, 64)
 
     def student_forward():
-        loop(0, 16, lambda i: pltpu.make_async_copy(w_in, wland.at[i], w_r.at[i]).wait())
+        loop(0, 16, lambda i: pltpu.make_async_copy(w_pad, wland.at[i], w_r.at[i]).wait())
         wz[...] = jnp.zeros_like(wz)
         bias = jnp.zeros((1, 1024), F32)
         for a in range(4):
@@ -239,36 +277,56 @@
         brow[...] = bias
         local[4].wait()
 
-        def one(i):
-            j = lax.rem(m + i, 8)
-
-            @pl.when(i > 0)
+        def fetch(j):
+            @pl.when(j != m)
             def _():
                 rcopy(xland.at[j], xland.at[j], x_s.at[0], x_r.at[j], g, sib).wait_recv()
 
-            xw = xland[j]
-            xt[j] = jnp.transpose(xw)
+            xt[j] = jnp.transpose(xland[j])
+
+        def one(i, j, dst):
+            fetch(j)
             for n in range(4):
                 cols = slice(n * 256, (n + 1) * 256)
-                o = jnp.dot(xw, wz[:, cols], preferred_element_type=F32) + brow[:, cols]
-                osend[j, :, cols] = o.astype(BF)
-
-            @pl.when(i > 0)
+                o = jnp.dot(xland[j], wz[:, cols], preferred_element_type=F32) + brow[:, cols]
+                dst[i, :, cols] = o.astype(BF)
+
+        def theirs(i):
+            xx = lax.rem(x + i, 4)
+            one(xx, (1 - core) * 4 + xx, osib)
+            os_send(xx, True)
+
+        loop(0, 4, theirs)
+        loop(0, 4, lambda i: one(i, core * 4 + i, osend))
+
+    def output_sums():
+        def one(i):
+            xx = lax.rem(x + i, 4)
+            rcopy(oswap.at[xx], oswap.at[xx], os_s.at[0], os_r.at[xx], g, sib).wait_recv()
+            osend[xx] = (osend[xx].astype(F32) + oswap[xx].astype(F32)).astype(BF)
+
+            @pl.when(i < 4)
             def _():
                 o_send(i, True)
 
-        loop(0, 8, one)
-        oland[m] = osend[m]
+        loop(1, 5, one)
+        oland[x] = osend[x]
 
     local[3].wait()
     pcopy.wait_recv()
 
     def chunk(i):
-        c = lax.rem(chip + 1 + i, 8)
-
-        @pl.when(i == 3)
+        z = lax.rem(cz + 1 + i // 2, 4)
+        own = lax.rem(i, 2) == 1
+        c = z * 2 + lax.rem(ch + 1 + i, 2)
+
+        @pl.when(i == 2)
         def _():
             student_forward()
+
+        @pl.when(i == 4)
+        def _():
+            output_sums()
 
         attend(core, c, qo.at[c], qs.at[c], keys, values, S, mx, acc, att)
         for n in range(4):
@@ -277,24 +335,48 @@
             p = p + jnp.dot(att[:, 512:], proj_s[:, cols], preferred_element_type=F32)
             tsend[c, :, cols] = p.astype(BF)
 
-        @pl.when(i < 7)
-        def _():
-            t_send(c, True)
+        @pl.when(i < 6)
+        def _():
+            ta_send(c, True)
+
+        @pl.when(jnp.logical_not(own))
+        def _():
+            tb_send(z, True)
+
+        @pl.when(own)
+        def _():
+            rcopy(tb.at[z], tb.at[z], tb_s.at[0], tb_r.at[z], g, sib).wait_recv()
+            tbsum[z] = (tsend[c, :, B].astype(F32) + tb[z].astype(F32)).astype(BF)
+
+            @pl.when(i < 6)
+            def _():
+                tb2_send(z, True)
+
+        @pl.when(i == 6)
+        def _():
+            total = tsend[c, :, A].astype(F32)
+            for k in range(1, 4):
+                zz = lax.rem(cz + k, 4)
+                ta_wait(1 - ch, zz)
+                total = total + ta[1 - ch, zz].astype(F32)
+            ta2[0] = total.astype(BF)
+            ta2_send().start()
 
     loop(0, 8, chunk)
-    tland[chip] = tsend[chip]
-
-    def t_wait(i):
-        q = lax.rem(chip + i, 8)
-        rcopy(tland.at[q], tland.at[q], t_s.at[0], t_r.at[q], g, sib).wait_recv()
-
-    loop(1, 8, t_wait)
-    for n in range(4):
-        cols = slice(n * 256, (n + 1) * 256)
-        total = tland[0, :, cols].astype(F32)
-        for q in range(1, 8):
-            total = total + tland[q, :, cols].astype(F32)
-        tsum[:, :, cols] = total.astype(BF).reshape(8, 16, 256)
+    total = tsend[chip, :, A].astype(F32)
+    for k in range(1, 4):
+        zz = lax.rem(cz + k, 4)
+        ta_wait(ch, zz)
+        total = total + ta[ch, zz].astype(F32)
+    ta2_send().wait_recv()
+    total = total + ta2[1].astype(F32)
+    tsum[:, :, A] = total.astype(BF).reshape(8, 16, 512)
+    total = tbsum[cz].astype(F32)
+    for k in range(1, 4):
+        zz = lax.rem(cz + k, 4)
+        rcopy(tb2.at[zz], tb2.at[zz], tb2_s.at[0], tb2_r.at[zz], g, sib).wait_recv()
+        total = total + tb2[zz].astype(F32)
+    tsum[:, :, B] = total.astype(BF).reshape(8, 16, 512)
 
     def p_send(i, start):
         j = lax.rem(g + i, 8)
@@ -308,10 +390,10 @@
     pland[g] = tsum[g]
 
     def o_wait(i):
-        j = lax.rem(m + i, 8)
+        j = lax.rem(x + i, 4)
         rcopy(oland.at[j], oland.at[j], o_s.at[0], o_r.at[j], g, sib).wait_recv()
 
-    loop(1, 8, o_wait)
+    loop(1, 4, o_wait)
 
     def p_wait(i):
         j = lax.rem(g + i, 8)
@@ -323,7 +405,7 @@
     for k in range(8):
         rows = slice(k * 16, (k + 1) * 16)
         o = oland[0, rows, :].astype(F32)
-        for j in range(1, 8):
+        for j in range(1, 4):
             o = o + oland[j, rows, :].astype(F32)
         paired = pland[own_in[k]].astype(F32)
         kk = jnp.concatenate([keep[rows]] * 8, axis=1)
@@ -427,24 +509,17 @@
         wsend[i] = v.astype(BF)
     loop(0, 16, lambda i: g_send(lax.rem(t + i, 16), True))
     loop(1, 9, input_grad)
-    igland[m] = igsend[m]
+    ig_own = pltpu.make_async_copy(igsend.at[m], igland.at[m], i_r.at[m])
+    ig_own.start()
 
     loop(0, 16, lambda i: pltpu.make_async_copy(wsend.at[i], wgland.at[i], g_r.at[i]).wait())
-    total = wgland[0].astype(F32)
-    for i in range(1, 16):
-        total = total + wgland[i].astype(F32)
-    wg_out[...] = total[:28]
-    small_out[...] = total[24:32]
+    ig_own.wait()
 
     def i_wait(i):
         j = lax.rem(m + i, 8)
         rcopy(igland.at[j], igland.at[j], i_s.at[0], i_r.at[j], g, sib).wait_recv()
 
     loop(1, 8, i_wait)
-    for b in range(4):
-        ig_out[:, b * 896:b * 896 + 384] = igland[2 * b, :, :384]
-        ig_out[:, b * 896 + 384:b * 896 + 512] = igland[2 * b, :, 384:] + igland[2 * b + 1, :, :128]
-        ig_out[:, b * 896 + 512:(b + 1) * 896] = igland[2 * b + 1, :, 128:]
 
     loop(1, 8, lambda i: kv_send(i, False))
     qcopy.wait_send()
@@ -452,8 +527,12 @@
     loop(0, 8, lambda i: kv_relay(i * 2 + core, False))
     loop(0, 16, lambda i: w_send(i, False))
     loop(1, 8, lambda i: x_send(i, False))
-    loop(1, 8, lambda i: o_send(i, False))
-    loop(1, 8, lambda i: t_send(lax.rem(chip + i, 8), False))
+    loop(0, 4, lambda i: os_send(i, False))
+    loop(1, 4, lambda i: o_send(i, False))
+    loop(2, 8, lambda i: ta_send(lax.rem(cz * 2 + i, 8), False))
+    loop(0, 4, lambda i: tb_send(i, False))
+    loop(1, 4, lambda i: tb2_send(lax.rem(cz + i, 4), False))
+    ta2_send().wait_send()
     loop(1, 8, lambda i: p_send(i, False))
     loop(1, 4, lambda i: e_send(i, False))
     loop(0, 4, lambda i: e_relay(i, False))
@@ -461,43 +540,64 @@
     loop(1, 8, lambda i: i_send(i, False))
 
 
+def finish(wgland, igland, wg_out, bias_out, loss_out, ig_out):
+    d = lax.axis_index("grp") * 16 + lax.axis_index("tp")
+    total = wgland[0].astype(F32)
+    for i in range(1, 16):
+        total = total + wgland[i].astype(F32)
+    wg_out[...] = total[:28]
+    small = total[24:32]
+    loss_out[...] = jnp.sum(small[6:8], axis=(0, 1), keepdims=True) / 32768.0
+    both = jnp.broadcast_to(small[4:5] + small[5:6], (8, 1024))
+    both = pltpu.roll(both, lax.rem(1024 - d * 8, 1024), 1)
+    bias_out[...] = both[0:1, 0:8]
+    for b in range(4):
+        ig_out[:, b * 896:b * 896 + 384] = igland[2 * b, :, :384]
+        ig_out[:, b * 896 + 384:b * 896 + 512] = igland[2 * b, :, 384:] + igland[2 * b + 1, :, :128]
+        ig_out[:, b * 896 + 512:(b + 1) * 896] = igland[2 * b + 1, :, 128:]
+
+
 def on_device(queries, keys_values, projector, ownership, token_ids, student_input, student_weight, student_bias):
-    d = lax.axis_index("grp") * 16 + lax.axis_index("tp")
-    bias_row = lax.dynamic_update_slice(jnp.zeros((4, 1024), BF), student_bias[None], (0, d * 8))
-    w_pad = jnp.concatenate([student_weight, bias_row], axis=0)
     hbm = pl.BlockSpec(memory_space=pl.ANY)
     vmem = pl.BlockSpec(memory_space=pltpu.VMEM)
     smem = pl.BlockSpec(memory_space=pltpu.SMEM)
     dma = pltpu.SemaphoreType.DMA
     V = pltpu.VMEM
-    wg, small, ig = pl.pallas_call(
+    wgland, igland = pl.pallas_call(
         kernel,
-        out_shape=(jax.ShapeDtypeStruct((28, 1024), F32), jax.ShapeDtypeStruct((8, 1024), F32),
-                   jax.ShapeDtypeStruct((128, 3584), BF)),
-        in_specs=[hbm, hbm, hbm, smem, vmem, hbm, hbm],
-        out_specs=(vmem, vmem, vmem),
+        out_shape=(jax.ShapeDtypeStruct((16, 32, 1024), BF), jax.ShapeDtypeStruct((8, 128, 512), BF)),
+        in_specs=[hbm, hbm, hbm, smem, vmem, hbm, vmem, vmem],
+        out_specs=(hbm, hbm),
         scratch_shapes=[
             V((8, 128, 512), BF), V((8, 128, 512), BF), V((2048, 128), BF), V((2048, 128), BF),
             V((1024, 2048), F32), V((1024, 128), F32), V((1024, 256), F32), V((128, 1024), BF),
-            V((512, 1024), BF), V((512, 1024), BF), V((8, 128, 1024), BF), V((8, 128, 1024), BF),
-            V((8, 16, 1024), BF), V((8, 16, 1024), BF),
-            V((8, 128, 512), BF), V((8, 512, 128), BF), V((16, 32, 1024), BF), V((512, 1024), BF), V((1, 1024), F32),
-            V((8, 128, 1024), BF), V((8, 128, 1024), BF), V((8, 128, 1024), BF),
-            V((512, 1024), F32), V((16, 32, 1024), BF), V((16, 32, 1024), BF),
-            V((8, 128, 512), BF), V((8, 128, 512), BF),
+            V((512, 1024), BF), V((512, 1024), BF), V((8, 128, 1024), BF),
+            V((2, 4, 128, 512), BF), V((2, 128, 512), BF), V((4, 128, 512), BF), V((4, 128, 512), BF),
+            V((4, 128, 512), BF), V((8, 16, 1024), BF), V((8, 16, 1024), BF),
+            V((8, 128, 512), BF), V((8, 512, 128), BF), V((32, 1024), BF), V((16, 32, 1024), BF),
+            V((512, 1024), BF), V((1, 1024), F32),
+            V((4, 128, 1024), BF), V((4, 128, 1024), BF), V((4, 128, 1024), BF), V((4, 128, 1024), BF),
+            V((8, 128, 1024), BF), V((512, 1024), F32), V((16, 32, 1024), BF), V((8, 128, 512), BF),
             dma((5,)), dma((2,)), dma((2,)), dma((8,)), dma((16,)), dma((8,)), dma((16,)), dma((8,)), dma((8,)),
-            dma((16,)), dma((16,)), dma((8,)), dma((8,)), dma((8,)), dma((8,)),
-            dma((8,)), dma((8,)), dma((8,)), dma((8,)), dma((4,)), dma((8,)), dma((4,)), dma((16,)), dma((16,)),
+            dma((16,)), dma((16,)), dma((8,)), dma((8,)), dma((4,)), dma((4,)), dma((4,)), dma((4,)),
+            dma((8,)), dma((8,)), dma((4,)), dma((4,)), dma((1,)), dma((1,)), dma((4,)), dma((4,)),
+            dma((8,)), dma((8,)), dma((4,)), dma((8,)), dma((4,)), dma((16,)), dma((16,)),
             dma((8,)), dma((8,)),
         ],
         compiler_params=pltpu.CompilerParams(
             collective_id=0, has_side_effects=True, vmem_limit_bytes=60 * 2 ** 20),
         cost_estimate=pl.CostEstimate(flops=9 * 10 ** 9, bytes_accessed=8 * 10 ** 6, transcendentals=9 * 10 ** 6),
     )(queries.reshape(8, 2, 128, 512), keys_values[0], projector, ownership, token_ids.reshape(1, 128),
-      student_input, w_pad)
-    loss = (jnp.sum(small[6]) + jnp.sum(small[7])) / 32768.0
-    bias = lax.dynamic_slice(small[4] + small[5], (d * 8,), (8,))
-    return loss, wg, bias, ig
+      student_input, student_weight, student_bias.reshape(1, 8))
+    wg, bias, loss, ig = pl.pallas_call(
+        finish,
+        out_shape=(jax.ShapeDtypeStruct((28, 1024), F32), jax.ShapeDtypeStruct((1, 8), F32),
+                   jax.ShapeDtypeStruct((1, 1), F32), jax.ShapeDtypeStruct((128, 3584), BF)),
+        in_specs=[vmem, vmem],
+        out_specs=(vmem, vmem, vmem, vmem),
+        compiler_params=pltpu.CompilerParams(vmem_limit_bytes=32 * 2 ** 20),
+    )(wgland, igland)
+    return loss.reshape(()), wg, bias.reshape(8), ig
 
 
 def solution(mesh):

time: 124 us -> 113 us (0.911); the launches traced: 122 us -> 113 us
  other arithmetic: 3.6 us -> 0 us
  between operations: 3.09 us -> 0.65 us
  local copies, waits for them, and re-layouts: 4.64 us -> 2.44 us
    reduce_sum x1 -> x0, other arithmetic: 1.53 us -> none  [on_device(): loss = (jnp.sum(small[6]) + jnp.sum(small[7])) / 32768.0]
    concatenate x1 -> x0, other arithmetic: 1.48 us -> none  [on_device(): w_pad = jnp.concatenate([student_weight, bias_row], axis=0)]
    unnamed x2 -> x4, local copies, waits for them, and re-layouts: 3.73 us -> 2.44 us
    pallas_call x1 -> x2, Pallas kernels: 111 us -> 110 us  [the longest x1 109 us: on_device(): pl.pallas_call(kernel, out_shape=(jax.ShapeDtypeStruct((16, 32, 1024), BF...]
where the time goes in v2:
time: 113 us
  Pallas kernels  110 us (97%)
  local copies, waits for them, and re-layouts  2.44 us (2%)
    pallas_call x1, Pallas kernels, on_device(): pl.pallas_call(kernel, out_shape=(jax.ShapeDtypeStruct((16, 32, 1024), BF...  109 us
    unnamed x4, local copies, waits for them, and re-layouts  2.44 us

profile of v2, /device:TPU:1, one launch (start us, length us, event | category | flops | bytes accessed | tf_op | source)
XLA Modules:
  0.0 113.3 jit_solution(16889514541004185181)
XLA Ops:
  0.6 109.0 %shard_map.111 = (bf16[16,32,1024]{2,1,0:T(8,128)(2,1)}, bf16[8,128,512]{2,1,0:T(8,128)(2,1)}) custom-call(bf16[8,2,128,512]{3,2,1,0:T(8,128)(2,1)} %bitcast.6, bf16[128,2048]{1,0:T(8,128)(2,1)} %bitcast.7, bf16[512,1024]{1,0:T(8,128)(2,1)} %proj_in.1, s32[8]{0:T(128)} %own_in.1, s32[1,128]{1,0:T(1,128)} %bitcast.8, bf16[128,3584]{1,0:T(8,128)(2,1)} %x_in.1, ...), custom_call_target="tpu_custom_call" | custom-call | flops 8999999488 | bytes 8000000 | tf_op jit(solution)/shard_map/pallas_call | solution.py:566
  109.6 0.0 copy-start
  109.6 1.2 %copy-done = bf16[16,32,1024]{2,1,0:T(8,128)(2,1)S(1)} copy-done((bf16[16,32,1024]{2,1,0:T(8,128)(2,1)S(1)}, bf16[16,32,1024]{2,1,0:T(8,128)(2,1)}, u32[]{:S(2)}) %copy-start) | copy-done | bytes 1048600
  110.9 0.0 copy-start.1
  110.9 1.2 %copy-done.1 = bf16[8,128,512]{2,1,0:T(8,128)(2,1)S(1)} copy-done((bf16[8,128,512]{2,1,0:T(8,128)(2,1)S(1)}, bf16[8,128,512]{2,1,0:T(8,128)(2,1)}, u32[]{:S(2)}) %copy-start.1) | copy-done | bytes 1048600
  112.1 1.2 %shard_map.112 = (f32[28,1024]{1,0:T(8,128)}, f32[1,8]{1,0:T(1,128)}, f32[1,1]{1,0:T(1,128)}, bf16[128,3584]{1,0:T(8,128)(2,1)}) custom-call(bf16[16,32,1024]{2,1,0:T(8,128)(2,1)S(1)} %copy-done, bf16[8,128,512]{2,1,0:T(8,128)(2,1)S(1)} %copy-done.1), custom_call_target="tpu_custom_call" | custom-call | tf_op jit(solution)/shard_map/pallas_call | solution.py:592
Async XLA Ops:
  109.6 1.2 %copy-start = (bf16[16,32,1024]{2,1,0:T(8,128)(2,1)S(1)}, bf16[16,32,1024]{2,1,0:T(8,128)(2,1)}, u32[]{:S(2)}) copy-start(bf16[16,32,1024]{2,1,0:T(8,128)(2,1)} %get-tuple-element.10.wgland) | copy-start | bytes 3145732
  110.9 1.2 %copy-start.1 = (bf16[8,128,512]{2,1,0:T(8,128)(2,1)S(1)}, bf16[8,128,512]{2,1,0:T(8,128)(2,1)}, u32[]{:S(2)}) copy-start(bf16[8,128,512]{2,1,0:T(8,128)(2,1)} %get-tuple-element.11.igland) | copy-start | bytes 3145732

commit v3 on v2

--- a/solution.py
+++ b/solution.py
@@ -24,47 +24,51 @@
     lax.fori_loop(first, last, lambda i, carry: (body(i), carry)[1], 0)
 
 
-def attend(core, c, qo, qs, keys, values, S, mx, acc, out):
-    T = 256
-
-    def score(j, masked):
-        at = pl.ds(pl.multiple_of(j * T, T), T)
-        kt = keys[at, :]
+def attend(core, c, qo, qs, keys, values, S, mx, acc, out, between):
+    q = jnp.concatenate([r[:, h * 128:(h + 1) * 128] for r in (qo, qs) for h in range(4)], axis=0)
+
+    def score(j, T, masked):
+        at = pl.ds(pl.multiple_of(j * 256, 256), T)
         if masked:
             row = lax.broadcasted_iota(jnp.int32, (128, T), 0) + core * 128
             keep = row >= lax.broadcasted_iota(jnp.int32, (128, T), 1)
+        s_all = lax.dot_general(q, keys[at, :], (((1,), (1,)), ((), ())), preferred_element_type=F32)
         for h in range(8):
             hr = slice(h * 128, (h + 1) * 128)
-            q = (qo if h < 4 else qs)[:, (h % 4) * 128:(h % 4) * 128 + 128]
-            s = lax.dot_general(q, kt, (((1,), (1,)), ((), ())), preferred_element_type=F32)
+            s = s_all[hr]
             if masked:
                 s = jnp.where(keep, s, -1e30)
             S[hr, at] = s
-            m = jnp.maximum(mx[hr, :], jnp.maximum(s[:, :128], s[:, 128:]))
+            m = mx[hr, :]
+            for w in range(T // 128):
+                m = jnp.maximum(m, s[:, w * 128:(w + 1) * 128])
             if masked:
                 m = jnp.broadcast_to(jnp.max(m, axis=1, keepdims=True) * SCALE, (128, 128))
             mx[hr, :] = m
 
     mx[...] = jnp.full_like(mx, -1e30)
-    loop(0, c, lambda j: score(j, False))
-    score(c, True)
+    loop(0, c // 2, lambda j: score(2 * j, 512, False))
+    loop(0, lax.rem(c, 2), lambda j: score(c - 1, 256, False))
+    score(c, 256, True)
     acc[...] = jnp.zeros_like(acc)
+    between()
 
     def weigh(off, W):
         vt = values[pl.ds(off, W), :]
         vt = jnp.concatenate([vt, jnp.ones_like(vt)], axis=1)
+        ps = []
         for h in range(8):
             hr = slice(h * 128, (h + 1) * 128)
             m = mx[hr, :]
-            ps = []
-            for w in range(W // 128):
-                s = S[hr, pl.ds(pl.multiple_of(off + w * 128, 128), 128)]
-                ps.append(jnp.exp2(s * SCALE - m).astype(BF))
-            acc[hr, :] += jnp.dot(jnp.concatenate(ps, axis=1), vt, preferred_element_type=F32)
+            ps.append(jnp.concatenate(
+                [jnp.exp2(S[hr, pl.ds(pl.multiple_of(off + w * 128, 128), 128)] * SCALE - m).astype(BF)
+                 for w in range(W // 128)], axis=1))
+        acc[...] += jnp.dot(jnp.concatenate(ps, axis=0), vt, preferred_element_type=F32)
 
     n = c + 1
-    loop(0, n // 2, lambda j: weigh(pl.multiple_of(j * 512, 512), 512))
-    loop(0, n % 2, lambda j: weigh(pl.multiple_of((n - 1) * 256, 256), 256))
+    loop(0, n // 4, lambda j: weigh(pl.multiple_of(j * 1024, 1024), 1024))
+    loop(0, lax.rem(n // 2, 2), lambda j: weigh(pl.multiple_of(n // 4 * 1024, 512), 512))
+    loop(0, lax.rem(n, 2), lambda j: weigh(pl.multiple_of((n - 1) * 256, 256), 256))
     for h in range(8):
         a = acc[h * 128:(h + 1) * 128, :]
         out[:, h * 128:(h + 1) * 128] = (a[:, :128] / a[:, 128:]).astype(BF)
@@ -73,9 +77,9 @@
 def kernel(q_in, kv_in, proj_in, own_in, ids_in, x_in, w_in, b_in,
            wgland, igland,
            qo, qs, keys, values, S, mx, acc, att, proj_o, proj_s, tsend, ta, ta2, tb, tbsum, tb2, tsum, pland,
-           xland, xt, w_pad, wland, wz, brow, osib, oswap, osend, oland, eland, wg, wsend, igsend,
+           xland, xt, w_pad, wland, wz, wz2, brow, osib, oswap, osend, oland, eland, wg, extra, wsend, igsend,
            l_sem, qp_s, qp_r, k_s, k_r, v_s, v_r, rk_s, rv_s, w_s, w_r, x_s, x_r, os_s, os_r, o_s, o_r,
-           ta_s, ta_r, tb_s, tb_r, ta2_s, ta2_r, tb2_s, tb2_r, p_s, p_r, e_s, e_r, re_s, g_s, g_r, i_s, i_r):
+           ta_s, ta_r, tb_s, tb_r, ta2_s, ta2_r, tb2_s, tb2_r, p_s, p_r, e_s, e_r, f_s, f_r, re_s, re_r, g_s, g_r, i_s, i_r, w2_s, w2_r, round2, round3):
     g = lax.axis_index("grp")
     t = lax.axis_index("tp")
     x, yl = lax.rem(g, 4), g // 4
@@ -116,64 +120,73 @@
 
     barrier = pltpu.get_barrier_semaphore()
 
-    def greet(grp, tp):
-        pl.semaphore_signal(barrier, inc=1, device_id=(grp, tp), device_id_type=MESH)
-
-    def greet_plane(i):
-        j = lax.rem(yl * 16 + t + i, 32)
-        greet((j // 16) * 4 + x, lax.rem(j, 16))
-
-    loop(1, 32, greet_plane)
-
-    def greet_x(i):
-        xx = lax.rem(x + i, 4)
-        greet(yl * 4 + xx, t)
-        greet(yl * 4 + xx, sib)
-        greet((1 - yl) * 4 + xx, t)
-
-    loop(1, 4, greet_x)
-    pl.semaphore_wait(barrier, 31 + 9)
+    def greet(sem):
+        def tell(grp, tp):
+            pl.semaphore_signal(sem, inc=1, device_id=(grp, tp), device_id_type=MESH)
+
+        loop(1, 8, lambda i: tell(g, lax.rem(chip + i, 8) * 2 + core))
+        tell(g, sib)
+        loop(1, 4, lambda i: tell(yl * 4 + lax.rem(x + i, 4), t))
+        tell((1 - yl) * 4 + x, t)
+
+    greet(barrier)
+    pl.semaphore_wait(barrier, 12)
 
     def kv_cols(q):
         return (pl.ds(pl.multiple_of(q * 128, 128), 128),
                 pl.ds(pl.multiple_of(1024 + q * 128, 128), 128))
 
-    def kv_send(i, start):
+    def k_send(i, start):
         q = lax.rem(chip + i, 8)
-        kc, vc = kv_cols(q)
-        a = rcopy(kv_in.at[:, kc], keys.at[own_kv, :], k_s.at[q], k_r.at[t], g, q * 2 + core)
-        b = rcopy(kv_in.at[:, vc], values.at[own_kv, :], v_s.at[q], v_r.at[t], g, q * 2 + core)
+        a = rcopy(kv_in.at[:, kv_cols(q)[0]], keys.at[own_kv, :], k_s.at[q], k_r.at[t], g, q * 2 + core)
         if start:
             a.start()
-            b.start()
         else:
             a.wait_send()
-            b.wait_send()
-
-    loop(1, 8, lambda i: kv_send(i, True))
+
+    def v_send(i, start):
+        q = lax.rem(chip + i, 8)
+        a = rcopy(kv_in.at[:, kv_cols(q)[1]], values.at[own_kv, :], v_s.at[q], v_r.at[t], g, q * 2 + core)
+        if start:
+            a.start()
+        else:
+            a.wait_send()
+
+    loop(1, 8, lambda i: k_send(i, True))
     qcopy = rcopy(q_in.at[:, 1 - core], qs, qp_s.at[0], qp_r.at[0], g, sib)
     pcopy = rcopy(proj_in, proj_s, qp_s.at[1], qp_r.at[1], g, sib)
     qcopy.start()
-
-    def kv_relay(src, start):
-        rows = pl.ds(pl.multiple_of(src * 128, 128), 128)
-        a = rcopy(keys.at[rows, :], keys.at[rows, :], rk_s.at[src // 2], k_r.at[src], g, sib)
-        b = rcopy(values.at[rows, :], values.at[rows, :], rv_s.at[src // 2], v_r.at[src], g, sib)
-        if start:
-            a.start()
-            b.start()
-        else:
-            a.wait_send()
-            b.wait_send()
-
-    def kv_wait(src):
-        rows = pl.ds(pl.multiple_of(src * 128, 128), 128)
-        rcopy(keys.at[rows, :], keys.at[rows, :], k_s.at[0], k_r.at[src], g, sib).wait_recv()
-        rcopy(values.at[rows, :], values.at[rows, :], v_s.at[0], v_r.at[src], g, sib).wait_recv()
+    loop(1, 8, lambda i: v_send(i, True))
+    greet(round2)
+
+    def rows_of(src):
+        return pl.ds(pl.multiple_of(src * 128, 128), 128)
+
+    def k_relay(src):
+        rows = rows_of(src)
+        return rcopy(keys.at[rows, :], keys.at[rows, :], rk_s.at[src // 2], k_r.at[src], g, sib)
+
+    def v_relay(src):
+        rows = rows_of(src)
+        return rcopy(values.at[rows, :], values.at[rows, :], rv_s.at[src // 2], v_r.at[src], g, sib)
+
+    def k_pass(i):
+        src = lax.rem(chip + 8 - i, 8) * 2 + core
+        k_relay(src).wait_recv()
+        k_relay(src).start()
+
+    def v_pass(i):
+        src = lax.rem(chip + 8 - i, 8) * 2 + core
+        v_relay(src).wait_recv()
+        v_relay(src).start()
 
     local[0].wait()
+    k_relay(t).start()
     local[1].wait()
-    kv_relay(t, True)
+    v_relay(t).start()
+    loop(1, 8, k_pass)
+    pl.semaphore_wait(round2, 12)
+    pl.semaphore_signal(round3, inc=1, device_id=(g, sib), device_id_type=MESH)
 
     def w_send(i, start):
         i = lax.rem(src16 + i, 16)
@@ -202,17 +215,12 @@
         else:
             copy.wait_send()
 
-    def kv_pass(i):
-        src = lax.rem(chip + 8 - i, 8) * 2 + core
-        kv_wait(src)
-        kv_relay(src, True)
-
-    loop(1, 8, kv_pass)
+    loop(1, 8, lambda i: x_send(i, True))
+    loop(1, 8, v_pass)
     pcopy.start()
+    pl.semaphore_wait(round3, 1)
     loop(0, 16, lambda i: w_send(i, True))
-    loop(1, 8, lambda i: x_send(i, True))
-
-    loop(0, 8, lambda i: kv_wait(i * 2 + 1 - core))
+    loop(0, 8, lambda i: k_relay(i * 2 + 1 - core).wait_recv())
     local[2].wait()
     qcopy.wait_recv()
 
@@ -311,9 +319,18 @@
 
         loop(1, 5, one)
         oland[x] = osend[x]
-
-    local[3].wait()
-    pcopy.wait_recv()
+        w2_send().start()
+
+    def w2_send():
+        return rcopy(wz, wz2, w2_s.at[0], w2_r.at[0], yl * 4 + lax.rem(x + 2, 4), t)
+
+    def first_chunk(i):
+        @pl.when(i == 0)
+        def _():
+            loop(0, 8, lambda k: v_relay(k * 2 + 1 - core).wait_recv())
+            local[3].wait()
+            pcopy.wait_recv()
+
 
     def chunk(i):
         z = lax.rem(cz + 1 + i // 2, 4)
@@ -328,7 +345,7 @@
         def _():
             output_sums()
 
-        attend(core, c, qo.at[c], qs.at[c], keys, values, S, mx, acc, att)
+        attend(core, c, qo.at[c], qs.at[c], keys, values, S, mx, acc, att, lambda: first_chunk(i))
         for n in range(4):
             cols = slice(n * 256, (n + 1) * 256)
             p = jnp.dot(att[:, :512], proj_o[:, cols], preferred_element_type=F32)
@@ -343,14 +360,12 @@
         def _():
             tb_send(z, True)
 
-        @pl.when(own)
-        def _():
-            rcopy(tb.at[z], tb.at[z], tb_s.at[0], tb_r.at[z], g, sib).wait_recv()
-            tbsum[z] = (tsend[c, :, B].astype(F32) + tb[z].astype(F32)).astype(BF)
-
-            @pl.when(i < 6)
-            def _():
-                tb2_send(z, True)
+        @pl.when((i > 0) & jnp.logical_not(own))
+        def _():
+            zz = lax.rem(cz + i // 2, 4)
+            rcopy(tb.at[zz], tb.at[zz], tb_s.at[0], tb_r.at[zz], g, sib).wait_recv()
+            tbsum[zz] = (tsend[zz * 2 + ch, :, B].astype(F32) + tb[zz].astype(F32)).astype(BF)
+            tb2_send(zz, True)
 
         @pl.when(i == 6)
         def _():
@@ -371,7 +386,8 @@
     ta2_send().wait_recv()
     total = total + ta2[1].astype(F32)
     tsum[:, :, A] = total.astype(BF).reshape(8, 16, 512)
-    total = tbsum[cz].astype(F32)
+    rcopy(tb.at[cz], tb.at[cz], tb_s.at[0], tb_r.at[cz], g, sib).wait_recv()
+    total = tsend[chip, :, B].astype(F32) + tb[cz].astype(F32)
     for k in range(1, 4):
         zz = lax.rem(cz + k, 4)
         rcopy(tb2.at[zz], tb2.at[zz], tb2_s.at[0], tb2_r.at[zz], g, sib).wait_recv()
@@ -411,120 +427,139 @@
         kk = jnp.concatenate([keep[rows]] * 8, axis=1)
         eland[m, rows, :] = (kk * (o - paired)).astype(BF)
 
-    def e_send(i, start):
-        xx = lax.rem(x + i, 4)
-        copy = rcopy(eland.at[m], eland.at[m], e_s.at[i], e_r.at[m], yl * 4 + xx, t)
-        if start:
-            copy.start()
-        else:
-            copy.wait_send()
-
-    def e_relay(i, start):
-        j = core * 4 + lax.rem(x + i, 4)
-        copy = rcopy(eland.at[j], eland.at[j], re_s.at[i], e_r.at[j], g, sib)
-        if start:
-            copy.start()
-        else:
-            copy.wait_send()
-
-    def e_wait(j):
-        rcopy(eland.at[j], eland.at[j], e_s.at[0], e_r.at[j], g, sib).wait_recv()
-
-    loop(1, 4, lambda i: e_send(i, True))
-    e_relay(0, True)
-
-    def e_pass(i):
-        e_wait(core * 4 + lax.rem(x + i, 4))
-        e_relay(i, True)
-
-    loop(1, 4, e_pass)
-    loop(0, 4, lambda i: e_wait((1 - core) * 4 + i))
-
-    def i_send(i, start):
-        j = lax.rem(m + i, 8)
-        dg, dt = member(j)
-        copy = rcopy(igsend.at[j], igland.at[m], i_s.at[j], i_r.at[m], dg, dt)
-        if start:
-            copy.start()
-        else:
-            copy.wait_send()
-
-    def input_grad(i):
-        j = lax.rem(m + i, 8)
-        igsend[j] = lax.dot_general(eland[j], wz[...], (((1,), (1,)), ((), ())),
-                                    preferred_element_type=F32).astype(BF)
-
-        @pl.when(i < 8)
-        def _():
-            i_send(i, True)
-
-    esum = []
-    lsum = []
-    for n in range(4):
-        cols = slice(n * 256, (n + 1) * 256)
-        total = jnp.zeros((512, 256), F32)
-        eb = jnp.zeros((8, 256), F32)
-        lb = jnp.zeros((8, 256), F32)
-        for j in range(8):
-            e = eland[j, :, cols]
-            total = total + jnp.dot(xt[j], e, preferred_element_type=F32)
-            ef = e.astype(F32)
-            for r in range(16):
-                er = ef[r * 8:(r + 1) * 8]
-                eb = eb + er
-                lb = lb + er * er
-        wg[:, cols] = total
-        esum.append(jnp.sum(eb, axis=0, keepdims=True))
-        lsum.append(jnp.sum(lb, axis=0, keepdims=True))
-    esum = jnp.concatenate(esum, axis=1)
-    lsum = jnp.concatenate(lsum, axis=1)
-    ehi = esum.astype(BF).astype(F32)
-    lhi = lsum.astype(BF).astype(F32)
-    extra = [ehi, esum - ehi, lhi, lsum - lhi]
-
-    def g_send(i, start):
-        here = (c_is_yl) & (i == t)
+    def cols_of(n):
+        return pl.ds(n * 512, 512)
+
+    def e_next(dx, k, n):
+        here = eland.at[m, :, cols_of(n)]
+        return rcopy(here, here, e_s.at[k * 2 + n], e_r.at[k * 2 + n], yl * 4 + lax.rem(x + dx, 4), t)
+
+    def e_far(dx, k, n):
+        here = eland.at[core * 4 + lax.rem(x + 4 - dx, 4), pl.ds(k * 64, 64), cols_of(n)]
+        return rcopy(here, here, f_s.at[k * 2 + n], f_r.at[k * 2 + n], yl * 4 + lax.rem(x + dx, 4), t)
+
+    def e_relay(dx, n):
+        xx = lax.rem(x + dx, 4)
+        here = eland.at[core * 4 + xx, :, cols_of(n)]
+        return rcopy(here, here, re_s.at[xx * 2 + n], re_r.at[xx * 2 + n], g, sib)
+
+    for n in range(2):
+        e_next(1, 0, n).start()
+        e_next(3, 1, n).start()
+        e_relay(0, n).start()
+
+    row = lax.broadcasted_iota(jnp.int32, (32, 512), 0)
+
+    def g_send(i, n, start):
+        here = (core == yl) & (i == t)
+        src, dst = wsend.at[i, :, cols_of(n)], wgland.at[src16, :, cols_of(n)]
 
         if start:
             @pl.when(here)
             def _():
-                pltpu.make_async_copy(wsend.at[i], wgland.at[src16], g_r.at[src16]).start()
+                pltpu.make_async_copy(src, dst, g_r.at[n * 16 + src16]).start()
 
         @pl.when(jnp.logical_not(here))
         def _():
-            copy = rcopy(wsend.at[i], wgland.at[src16], g_s.at[i], g_r.at[src16], core * 4 + x, i)
+            copy = rcopy(src, dst, g_s.at[n * 16 + i], g_r.at[n * 16 + src16], core * 4 + x, i)
             if start:
                 copy.start()
             else:
                 copy.wait_send()
 
-    c_is_yl = core == yl
-    row = lax.broadcasted_iota(jnp.int32, (32, 1024), 0)
-    for i in range(16):
-        v = wg[pl.ds(off + (28 * i) // 8 * 8, 32), :]
-        if (28 * i) % 8:
-            v = pltpu.roll(v, 28, 0)
-        for r in range(4):
-            v = jnp.where(row == 28 + r, extra[r], v)
-        wsend[i] = v.astype(BF)
-    loop(0, 16, lambda i: g_send(lax.rem(t + i, 16), True))
-    loop(1, 9, input_grad)
-    ig_own = pltpu.make_async_copy(igsend.at[m], igland.at[m], i_r.at[m])
-    ig_own.start()
-
-    loop(0, 16, lambda i: pltpu.make_async_copy(wsend.at[i], wgland.at[i], g_r.at[i]).wait())
-    ig_own.wait()
+    for n in range(2):
+        e_next(1, 0, n).wait_recv()
+        e_far(1, 0, n).start()
+        e_relay(3, n).start()
+        e_next(3, 1, n).wait_recv()
+        e_far(3, 1, n).start()
+        e_relay(1, n).start()
+        e_far(1, 0, n).wait_recv()
+        e_far(3, 1, n).wait_recv()
+        e_relay(2, n).start()
+        for k in range(4):
+            e_relay(k, n).wait_recv()
+
+        for u in range(2):
+            cols = slice(n * 512 + u * 256, n * 512 + (u + 1) * 256)
+            total = jnp.zeros((512, 256), F32)
+            eb = jnp.zeros((8, 256), F32)
+            lb = jnp.zeros((8, 256), F32)
+            for j in range(8):
+                e = eland[j, :, cols]
+                total = total + jnp.dot(xt[j], e, preferred_element_type=F32)
+                ef = e.astype(F32)
+                for r in range(16):
+                    er = ef[r * 8:(r + 1) * 8]
+                    eb = eb + er
+                    lb = lb + er * er
+            wg[:, cols] = total
+            esum = jnp.sum(eb, axis=0, keepdims=True)
+            lsum = jnp.sum(lb, axis=0, keepdims=True)
+            ehi = esum.astype(BF).astype(F32)
+            lhi = lsum.astype(BF).astype(F32)
+            for r, v in enumerate([ehi, esum - ehi, lhi, lsum - lhi]):
+                extra[r:r + 1, cols] = v
+        cols = slice(n * 512, (n + 1) * 512)
+        for i in range(16):
+            v = wg[pl.ds(off + (28 * i) // 8 * 8, 32), cols]
+            if (28 * i) % 8:
+                v = pltpu.roll(v, 28, 0)
+            for r in range(4):
+                v = jnp.where(row == 28 + r, extra[r:r + 1, cols], v)
+            wsend[i, :, cols] = v.astype(BF)
+        loop(0, 16, lambda i: g_send(lax.rem(t + i, 16), n, True))
+
+    m2 = core * 4 + lax.rem(x + 2, 4)
+
+    def i_send(k, j, slot, start):
+        dg, dt = member(j)
+        copy = rcopy(igsend.at[k], igland.at[slot], i_s.at[k], i_r.at[slot], dg, dt)
+        if start:
+            copy.start()
+        else:
+            copy.wait_send()
+
+    pairs = [(1, wz, m), (3, wz, m), (0, wz, m), (0, wz2, m2)]
+    ig_own = [pltpu.make_async_copy(igsend.at[4], igland.at[m], i_r.at[m]),
+              pltpu.make_async_copy(igsend.at[6], igland.at[m2], i_r.at[m2])]
+    for k, (dx, w, slot) in enumerate(pairs):
+        xx = lax.rem(x + dx, 4)
+        mine, other = core * 4 + xx, (1 - core) * 4 + xx
+        if k == 3:
+            w2_send().wait_recv()
+        e = jnp.concatenate([eland[mine], eland[other]], axis=0)
+        ig = lax.dot_general(e, w[...], (((1,), (1,)), ((), ())), preferred_element_type=F32).astype(BF)
+        igsend[2 * k] = ig[:128]
+        igsend[2 * k + 1] = ig[128:]
+        if dx:
+            i_send(2 * k, mine, slot, True)
+        else:
+            ig_own[k - 2].start()
+        i_send(2 * k + 1, other, slot, True)
+
+    def g_wait(i):
+        for n in range(2):
+            here = wgland.at[i, :, cols_of(n)]
+            pltpu.make_async_copy(wsend.at[i, :, cols_of(n)], here, g_r.at[n * 16 + i]).wait()
+
+    loop(0, 16, g_wait)
+    for copy in ig_own:
+        copy.wait()
 
     def i_wait(i):
-        j = lax.rem(m + i, 8)
-        rcopy(igland.at[j], igland.at[j], i_s.at[0], i_r.at[j], g, sib).wait_recv()
-
-    loop(1, 8, i_wait)
-
-    loop(1, 8, lambda i: kv_send(i, False))
+        @pl.when((i != m) & (i != m2))
+        def _():
+            rcopy(igland.at[i], igland.at[i], i_s.at[0], i_r.at[i], g, sib).wait_recv()
+
+    loop(0, 8, i_wait)
+    loop(1, 8, lambda i: k_send(i, False))
+    loop(1, 8, lambda i: v_send(i, False))
     qcopy.wait_send()
     pcopy.wait_send()
-    loop(0, 8, lambda i: kv_relay(i * 2 + core, False))
+    loop(0, 8, lambda i: k_relay(i * 2 + core).wait_send())
+    loop(0, 8, lambda i: v_relay(i * 2 + core).wait_send())
+    w2_send().wait_send()
     loop(0, 16, lambda i: w_send(i, False))
     loop(1, 8, lambda i: x_send(i, False))
     loop(0, 4, lambda i: os_send(i, False))
@@ -534,10 +569,18 @@
     loop(1, 4, lambda i: tb2_send(lax.rem(cz + i, 4), False))
     ta2_send().wait_send()
     loop(1, 8, lambda i: p_send(i, False))
-    loop(1, 4, lambda i: e_send(i, False))
-    loop(0, 4, lambda i: e_relay(i, False))
-    loop(0, 16, lambda i: g_send(i, False))
-    loop(1, 8, lambda i: i_send(i, False))
+    for n in range(2):
+        for k, dx in ((0, 1), (1, 3)):
+            e_next(dx, k, n).wait_send()
+            e_far(dx, k, n).wait_send()
+        for dx in range(4):
+            e_relay(dx, n).wait_send()
+        loop(0, 16, lambda i: g_send(i, n, False))
+    for k, (dx, w, slot) in enumerate(pairs):
+        xx = lax.rem(x + dx, 4)
+        if dx:
+            i_send(2 * k, core * 4 + xx, slot, False)
+        i_send(2 * k + 1, (1 - core) * 4 + xx, slot, False)
 
 
 def finish(wgland, igland, wg_out, bias_out, loss_out, ig_out):
@@ -575,14 +618,15 @@
             V((2, 4, 128, 512), BF), V((2, 128, 512), BF), V((4, 128, 512), BF), V((4, 128, 512), BF),
             V((4, 128, 512), BF), V((8, 16, 1024), BF), V((8, 16, 1024), BF),
             V((8, 128, 512), BF), V((8, 512, 128), BF), V((32, 1024), BF), V((16, 32, 1024), BF),
-            V((512, 1024), BF), V((1, 1024), F32),
+            V((512, 1024), BF), V((512, 1024), BF), V((1, 1024), F32),
             V((4, 128, 1024), BF), V((4, 128, 1024), BF), V((4, 128, 1024), BF), V((4, 128, 1024), BF),
-            V((8, 128, 1024), BF), V((512, 1024), F32), V((16, 32, 1024), BF), V((8, 128, 512), BF),
+            V((8, 128, 1024), BF), V((512, 1024), F32), V((8, 1024), F32), V((16, 32, 1024), BF), V((8, 128, 512), BF),
             dma((5,)), dma((2,)), dma((2,)), dma((8,)), dma((16,)), dma((8,)), dma((16,)), dma((8,)), dma((8,)),
             dma((16,)), dma((16,)), dma((8,)), dma((8,)), dma((4,)), dma((4,)), dma((4,)), dma((4,)),
             dma((8,)), dma((8,)), dma((4,)), dma((4,)), dma((1,)), dma((1,)), dma((4,)), dma((4,)),
-            dma((8,)), dma((8,)), dma((4,)), dma((8,)), dma((4,)), dma((16,)), dma((16,)),
-            dma((8,)), dma((8,)),
+            dma((8,)), dma((8,)), dma((4,)), dma((4,)), dma((4,)), dma((4,)), dma((8,)), dma((8,)),
+            dma((32,)), dma((32,)), dma((8,)), dma((8,)), dma((1,)), dma((1,)),
+            pltpu.SemaphoreType.REGULAR, pltpu.SemaphoreType.REGULAR,
         ],
         compiler_params=pltpu.CompilerParams(
             collective_id=0, has_side_effects=True, vmem_limit_bytes=60 * 2 ** 20),

time: 113 us -> 119 us (1.053)
  Pallas kernels: 110 us -> 116 us
    pallas_call x1, Pallas kernels: 109 us -> 114 us  [on_device(): pl.pallas_call(kernel, out_shape=(jax.ShapeDtypeStruct((16, 32, 1024), BF...]
where the time goes in v3:
time: 119 us
  Pallas kernels  116 us (97%)
  local copies, waits for them, and re-layouts  2.44 us (2%)
    pallas_call x1, Pallas kernels, on_device(): pl.pallas_call(kernel, out_shape=(jax.ShapeDtypeStruct((16, 32, 1024), BF...  114 us
    unnamed x4, local copies, waits for them, and re-layouts  2.44 us

profile of v3, /device:TPU:1, one launch (start us, length us, event | category | flops | bytes accessed | tf_op | source)
XLA Modules:
  0.0 118.8 jit_solution(11950603041741417197)
XLA Ops:
  0.6 114.5 %shard_map.111 = (bf16[16,32,1024]{2,1,0:T(8,128)(2,1)}, bf16[8,128,512]{2,1,0:T(8,128)(2,1)}) custom-call(bf16[8,2,128,512]{3,2,1,0:T(8,128)(2,1)} %bitcast.6, bf16[128,2048]{1,0:T(8,128)(2,1)} %bitcast.7, bf16[512,1024]{1,0:T(8,128)(2,1)} %proj_in.1, s32[8]{0:T(128)} %own_in.1, s32[1,128]{1,0:T(1,128)} %bitcast.8, bf16[128,3584]{1,0:T(8,128)(2,1)} %x_in.1, ...), custom_call_target="tpu_custom_call" | custom-call | flops 8999999488 | bytes 8000000 | tf_op jit(solution)/shard_map/pallas_call | solution.py:609
  115.1 0.0 copy-start
  115.1 1.2 %copy-done = bf16[16,32,1024]{2,1,0:T(8,128)(2,1)S(1)} copy-done((bf16[16,32,1024]{2,1,0:T(8,128)(2,1)S(1)}, bf16[16,32,1024]{2,1,0:T(8,128)(2,1)}, u32[]{:S(2)}) %copy-start) | copy-done | bytes 1048600
  116.4 0.0 copy-start.1
  116.4 1.2 %copy-done.1 = bf16[8,128,512]{2,1,0:T(8,128)(2,1)S(1)} copy-done((bf16[8,128,512]{2,1,0:T(8,128)(2,1)S(1)}, bf16[8,128,512]{2,1,0:T(8,128)(2,1)}, u32[]{:S(2)}) %copy-start.1) | copy-done | bytes 1048600
  117.6 1.2 %shard_map.112 = (f32[28,1024]{1,0:T(8,128)}, f32[1,8]{1,0:T(1,128)}, f32[1,1]{1,0:T(1,128)}, bf16[128,3584]{1,0:T(8,128)(2,1)}) custom-call(bf16[16,32,1024]{2,1,0:T(8,128)(2,1)S(1)} %copy-done, bf16[8,128,512]{2,1,0:T(8,128)(2,1)S(1)} %copy-done.1), custom_call_target="tpu_custom_call" | custom-call | tf_op jit(solution)/shard_map/pallas_call | solution.py:636
Async XLA Ops:
  115.1 1.2 %copy-start = (bf16[16,32,1024]{2,1,0:T(8,128)(2,1)S(1)}, bf16[16,32,1024]{2,1,0:T(8,128)(2,1)}, u32[]{:S(2)}) copy-start(bf16[16,32,1024]{2,1,0:T(8,128)(2,1)} %get-tuple-element.10.wgland) | copy-start | bytes 3145732
  116.4 1.2 %copy-start.1 = (bf16[8,128,512]{2,1,0:T(8,128)(2,1)S(1)}, bf16[8,128,512]{2,1,0:T(8,128)(2,1)}, u32[]{:S(2)}) copy-start(bf16[8,128,512]{2,1,0:T(8,128)(2,1)} %get-tuple-element.11.igland) | copy-start | bytes 3145732

commit v4 on v3

--- a/solution.py
+++ b/solution.py
@@ -77,9 +77,9 @@
 def kernel(q_in, kv_in, proj_in, own_in, ids_in, x_in, w_in, b_in,
            wgland, igland,
            qo, qs, keys, values, S, mx, acc, att, proj_o, proj_s, tsend, ta, ta2, tb, tbsum, tb2, tsum, pland,
-           xland, xt, w_pad, wland, wz, wz2, brow, osib, oswap, osend, oland, eland, wg, extra, wsend, igsend,
+           xland, xt, w_pad, wland, wz, brow, osib, oswap, osend, oland, eland, wg, wsend, igsend,
            l_sem, qp_s, qp_r, k_s, k_r, v_s, v_r, rk_s, rv_s, w_s, w_r, x_s, x_r, os_s, os_r, o_s, o_r,
-           ta_s, ta_r, tb_s, tb_r, ta2_s, ta2_r, tb2_s, tb2_r, p_s, p_r, e_s, e_r, f_s, f_r, re_s, re_r, g_s, g_r, i_s, i_r, w2_s, w2_r, round2, round3):
+           ta_s, ta_r, tb_s, tb_r, ta2_s, ta2_r, tb2_s, tb2_r, p_s, p_r, e_s, e_r, re_s, re_r, g_s, g_r, i_s, i_r, round2, round3):
     g = lax.axis_index("grp")
     t = lax.axis_index("tp")
     x, yl = lax.rem(g, 4), g // 4
@@ -137,7 +137,7 @@
                 pl.ds(pl.multiple_of(1024 + q * 128, 128), 128))
 
     def k_send(i, start):
-        q = lax.rem(chip + i, 8)
+        q = lax.rem(chip + i * (1 + 6 * core), 8)
         a = rcopy(kv_in.at[:, kv_cols(q)[0]], keys.at[own_kv, :], k_s.at[q], k_r.at[t], g, q * 2 + core)
         if start:
             a.start()
@@ -145,7 +145,7 @@
             a.wait_send()
 
     def v_send(i, start):
-        q = lax.rem(chip + i, 8)
+        q = lax.rem(chip + i * (1 + 6 * core), 8)
         a = rcopy(kv_in.at[:, kv_cols(q)[1]], values.at[own_kv, :], v_s.at[q], v_r.at[t], g, q * 2 + core)
         if start:
             a.start()
@@ -171,12 +171,12 @@
         return rcopy(values.at[rows, :], values.at[rows, :], rv_s.at[src // 2], v_r.at[src], g, sib)
 
     def k_pass(i):
-        src = lax.rem(chip + 8 - i, 8) * 2 + core
+        src = lax.rem(chip + i * (7 - 6 * core), 8) * 2 + core
         k_relay(src).wait_recv()
         k_relay(src).start()
 
     def v_pass(i):
-        src = lax.rem(chip + 8 - i, 8) * 2 + core
+        src = lax.rem(chip + i * (7 - 6 * core), 8) * 2 + core
         v_relay(src).wait_recv()
         v_relay(src).start()
 
@@ -290,7 +290,6 @@
             def _():
                 rcopy(xland.at[j], xland.at[j], x_s.at[0], x_r.at[j], g, sib).wait_recv()
 
-            xt[j] = jnp.transpose(xland[j])
 
         def one(i, j, dst):
             fetch(j)
@@ -319,10 +318,6 @@
 
         loop(1, 5, one)
         oland[x] = osend[x]
-        w2_send().start()
-
-    def w2_send():
-        return rcopy(wz, wz2, w2_s.at[0], w2_r.at[0], yl * 4 + lax.rem(x + 2, 4), t)
 
     def first_chunk(i):
         @pl.when(i == 0)
@@ -333,15 +328,16 @@
 
 
     def chunk(i):
-        z = lax.rem(cz + 1 + i // 2, 4)
-        own = lax.rem(i, 2) == 1
-        c = z * 2 + lax.rem(ch + 1 + i, 2)
-
-        @pl.when(i == 2)
+        k = jnp.where(i < 3, i + 1, jnp.where(i < 5, i - 2, jnp.where(i == 6, 3, 0)))
+        other = (i < 3) | (i == 5)
+        z = lax.rem(cz + k * (1 + 2 * core), 4)
+        c = z * 2 + lax.rem(ch + jnp.where(other, 1, 0), 2)
+
+        @pl.when(i == 4)
         def _():
             student_forward()
 
-        @pl.when(i == 4)
+        @pl.when(i == 6)
         def _():
             output_sums()
 
@@ -352,22 +348,21 @@
             p = p + jnp.dot(att[:, 512:], proj_s[:, cols], preferred_element_type=F32)
             tsend[c, :, cols] = p.astype(BF)
 
-        @pl.when(i < 6)
+        @pl.when(k > 0)
         def _():
             ta_send(c, True)
 
-        @pl.when(jnp.logical_not(own))
+        @pl.when(other)
         def _():
             tb_send(z, True)
 
-        @pl.when((i > 0) & jnp.logical_not(own))
-        def _():
-            zz = lax.rem(cz + i // 2, 4)
-            rcopy(tb.at[zz], tb.at[zz], tb_s.at[0], tb_r.at[zz], g, sib).wait_recv()
-            tbsum[zz] = (tsend[zz * 2 + ch, :, B].astype(F32) + tb[zz].astype(F32)).astype(BF)
-            tb2_send(zz, True)
-
-        @pl.when(i == 6)
+        @pl.when(jnp.logical_not(other) & (k > 0))
+        def _():
+            rcopy(tb.at[z], tb.at[z], tb_s.at[0], tb_r.at[z], g, sib).wait_recv()
+            tbsum[z] = (tsend[c, :, B].astype(F32) + tb[z].astype(F32)).astype(BF)
+            tb2_send(z, True)
+
+        @pl.when(i == 5)
         def _():
             total = tsend[c, :, A].astype(F32)
             for k in range(1, 4):
@@ -378,6 +373,8 @@
             ta2_send().start()
 
     loop(0, 8, chunk)
+    for j in range(8):
+        xt[:, j * 128:(j + 1) * 128] = jnp.transpose(xland[j])
     total = tsend[chip, :, A].astype(F32)
     for k in range(1, 4):
         zz = lax.rem(cz + k, 4)
@@ -418,37 +415,41 @@
     loop(1, 8, p_wait)
     keep = jnp.where(ids_in[...] < TEXT_IDS, 1.0, 0.0).astype(F32)
     keep = jnp.transpose(jnp.broadcast_to(keep, (128, 128)))
-    for k in range(8):
-        rows = slice(k * 16, (k + 1) * 16)
-        o = oland[0, rows, :].astype(F32)
-        for j in range(1, 4):
-            o = o + oland[j, rows, :].astype(F32)
-        paired = pland[own_in[k]].astype(F32)
-        kk = jnp.concatenate([keep[rows]] * 8, axis=1)
-        eland[m, rows, :] = (kk * (o - paired)).astype(BF)
+    keep = jnp.concatenate([keep, keep], axis=1)
+
+    def errors(n):
+        cols = slice(n * 256, (n + 1) * 256)
+        for k in range(8):
+            rows = slice(k * 16, (k + 1) * 16)
+            o = oland[0, rows, cols].astype(F32)
+            for j in range(1, 4):
+                o = o + oland[j, rows, cols].astype(F32)
+            eland[m, rows, cols] = (keep[rows] * (o - pland[own_in[k], :, cols].astype(F32))).astype(BF)
 
     def cols_of(n):
-        return pl.ds(n * 512, 512)
-
-    def e_next(dx, k, n):
+        return pl.ds(n * 256, 256)
+
+    def e_send(dx, n):
         here = eland.at[m, :, cols_of(n)]
-        return rcopy(here, here, e_s.at[k * 2 + n], e_r.at[k * 2 + n], yl * 4 + lax.rem(x + dx, 4), t)
-
-    def e_far(dx, k, n):
-        here = eland.at[core * 4 + lax.rem(x + 4 - dx, 4), pl.ds(k * 64, 64), cols_of(n)]
-        return rcopy(here, here, f_s.at[k * 2 + n], f_r.at[k * 2 + n], yl * 4 + lax.rem(x + dx, 4), t)
+        return rcopy(here, here, e_s.at[dx * 4 + n], e_r.at[dx * 4 + n], yl * 4 + lax.rem(x + dx, 4), t)
 
     def e_relay(dx, n):
         xx = lax.rem(x + dx, 4)
         here = eland.at[core * 4 + xx, :, cols_of(n)]
-        return rcopy(here, here, re_s.at[xx * 2 + n], re_r.at[xx * 2 + n], g, sib)
-
-    for n in range(2):
-        e_next(1, 0, n).start()
-        e_next(3, 1, n).start()
+        return rcopy(here, here, re_s.at[xx * 4 + n], re_r.at[xx * 4 + n], g, sib)
+
+    def e_begin(n):
+        errors(n)
+        for dx in (2, 1, 3):
+            e_send(dx, n).start()
         e_relay(0, n).start()
 
-    row = lax.broadcasted_iota(jnp.int32, (32, 512), 0)
+    def e_pass(n):
+        for dx in (1, 3, 2):
+            e_send(dx, n).wait_recv()
+            e_relay(4 - dx, n).start()
+
+    row = lax.broadcasted_iota(jnp.int32, (32, 256), 0)
 
     def g_send(i, n, start):
         here = (core == yl) & (i == t)
@@ -467,50 +468,41 @@
             else:
                 copy.wait_send()
 
-    for n in range(2):
-        e_next(1, 0, n).wait_recv()
-        e_far(1, 0, n).start()
-        e_relay(3, n).start()
-        e_next(3, 1, n).wait_recv()
-        e_far(3, 1, n).start()
-        e_relay(1, n).start()
-        e_far(1, 0, n).wait_recv()
-        e_far(3, 1, n).wait_recv()
-        e_relay(2, n).start()
-        for k in range(4):
-            e_relay(k, n).wait_recv()
-
-        for u in range(2):
-            cols = slice(n * 512 + u * 256, n * 512 + (u + 1) * 256)
-            total = jnp.zeros((512, 256), F32)
-            eb = jnp.zeros((8, 256), F32)
-            lb = jnp.zeros((8, 256), F32)
-            for j in range(8):
-                e = eland[j, :, cols]
-                total = total + jnp.dot(xt[j], e, preferred_element_type=F32)
-                ef = e.astype(F32)
-                for r in range(16):
-                    er = ef[r * 8:(r + 1) * 8]
-                    eb = eb + er
-                    lb = lb + er * er
-            wg[:, cols] = total
-            esum = jnp.sum(eb, axis=0, keepdims=True)
-            lsum = jnp.sum(lb, axis=0, keepdims=True)
-            ehi = esum.astype(BF).astype(F32)
-            lhi = lsum.astype(BF).astype(F32)
-            for r, v in enumerate([ehi, esum - ehi, lhi, lsum - lhi]):
-                extra[r:r + 1, cols] = v
-        cols = slice(n * 512, (n + 1) * 512)
+    def weight_grad(n):
+        if n < 3:
+            for k in range(4):
+                e_relay(k, n).wait_recv()
+        cols = slice(n * 256, (n + 1) * 256)
+        eb = jnp.zeros((8, 256), F32)
+        lb = jnp.zeros((8, 256), F32)
+        for j in range(8):
+            ef = eland[j, :, cols].astype(F32)
+            for r in range(16):
+                er = ef[r * 8:(r + 1) * 8]
+                eb = eb + er
+                lb = lb + er * er
+        wg[...] = jnp.dot(xt[...], eland[:, :, cols].reshape(1024, 256), preferred_element_type=F32)
+        esum = jnp.sum(eb, axis=0, keepdims=True)
+        lsum = jnp.sum(lb, axis=0, keepdims=True)
+        ehi = esum.astype(BF).astype(F32)
+        lhi = lsum.astype(BF).astype(F32)
         for i in range(16):
-            v = wg[pl.ds(off + (28 * i) // 8 * 8, 32), cols]
+            v = wg[pl.ds(off + (28 * i) // 8 * 8, 32), :]
             if (28 * i) % 8:
                 v = pltpu.roll(v, 28, 0)
-            for r in range(4):
-                v = jnp.where(row == 28 + r, extra[r:r + 1, cols], v)
+            for r, e in enumerate([ehi, esum - ehi, lhi, lsum - lhi]):
+                v = jnp.where(row == 28 + r, e, v)
             wsend[i, :, cols] = v.astype(BF)
         loop(0, 16, lambda i: g_send(lax.rem(t + i, 16), n, True))
 
-    m2 = core * 4 + lax.rem(x + 2, 4)
+    for n in range(4):
+        e_begin(n)
+    for n in range(3):
+        e_pass(n)
+        weight_grad(n)
+    e_pass(3)
+    for k in range(4):
+        e_relay(k, 3).wait_recv()
 
     def i_send(k, j, slot, start):
         dg, dt = member(j)
@@ -520,14 +512,13 @@
         else:
             copy.wait_send()
 
-    pairs = [(1, wz, m), (3, wz, m), (0, wz, m), (0, wz2, m2)]
-    ig_own = [pltpu.make_async_copy(igsend.at[4], igland.at[m], i_r.at[m]),
-              pltpu.make_async_copy(igsend.at[6], igland.at[m2], i_r.at[m2])]
+    pairs = [(2, wz, m), (1, wz, m), (3, wz, m), (0, wz, m)]
+    ig_own = [pltpu.make_async_copy(igsend.at[6], igland.at[m], i_r.at[m])]
     for k, (dx, w, slot) in enumerate(pairs):
+        if k == 3:
+            weight_grad(3)
         xx = lax.rem(x + dx, 4)
         mine, other = core * 4 + xx, (1 - core) * 4 + xx
-        if k == 3:
-            w2_send().wait_recv()
         e = jnp.concatenate([eland[mine], eland[other]], axis=0)
         ig = lax.dot_general(e, w[...], (((1,), (1,)), ((), ())), preferred_element_type=F32).astype(BF)
         igsend[2 * k] = ig[:128]
@@ -535,11 +526,11 @@
         if dx:
             i_send(2 * k, mine, slot, True)
         else:
-            ig_own[k - 2].start()
+            ig_own[0].start()
         i_send(2 * k + 1, other, slot, True)
 
     def g_wait(i):
-        for n in range(2):
+        for n in range(4):
             here = wgland.at[i, :, cols_of(n)]
             pltpu.make_async_copy(wsend.at[i, :, cols_of(n)], here, g_r.at[n * 16 + i]).wait()
 
@@ -548,7 +539,7 @@
         copy.wait()
 
     def i_wait(i):
-        @pl.when((i != m) & (i != m2))
+        @pl.when(i != m)
         def _():
             rcopy(igland.at[i], igland.at[i], i_s.at[0], i_r.at[i], g, sib).wait_recv()
 
@@ -559,7 +550,6 @@
     pcopy.wait_send()
     loop(0, 8, lambda i: k_relay(i * 2 + core).wait_send())
     loop(0, 8, lambda i: v_relay(i * 2 + core).wait_send())
-    w2_send().wait_send()
     loop(0, 16, lambda i: w_send(i, False))
     loop(1, 8, lambda i: x_send(i, False))
     loop(0, 4, lambda i: os_send(i, False))
@@ -569,10 +559,9 @@
     loop(1, 4, lambda i: tb2_send(lax.rem(cz + i, 4), False))
     ta2_send().wait_send()
     loop(1, 8, lambda i: p_send(i, False))
-    for n in range(2):
-        for k, dx in ((0, 1), (1, 3)):
-            e_next(dx, k, n).wait_send()
-            e_far(dx, k, n).wait_send()
+    for n in range(4):
+        for dx in (1, 2, 3):
+            e_send(dx, n).wait_send()
         for dx in range(4):
             e_relay(dx, n).wait_send()
         loop(0, 16, lambda i: g_send(i, n, False))
@@ -583,8 +572,13 @@
         i_send(2 * k + 1, (1 - core) * 4 + xx, slot, False)
 
 
-def finish(wgland, igland, wg_out, bias_out, loss_out, ig_out):
+def finish(wg_in, ig_in, wg_out, bias_out, loss_out, ig_out, wgland, igland, sem):
     d = lax.axis_index("grp") * 16 + lax.axis_index("tp")
+    wg_copy = pltpu.make_async_copy(wg_in, wgland, sem.at[0])
+    ig_copy = pltpu.make_async_copy(ig_in, igland, sem.at[1])
+    wg_copy.start()
+    ig_copy.start()
+    wg_copy.wait()
     total = wgland[0].astype(F32)
     for i in range(1, 16):
         total = total + wgland[i].astype(F32)
@@ -594,6 +588,7 @@
     both = jnp.broadcast_to(small[4:5] + small[5:6], (8, 1024))
     both = pltpu.roll(both, lax.rem(1024 - d * 8, 1024), 1)
     bias_out[...] = both[0:1, 0:8]
+    ig_copy.wait()
     for b in range(4):
         ig_out[:, b * 896:b * 896 + 384] = igland[2 * b, :, :384]
         ig_out[:, b * 896 + 384:b * 896 + 512] = igland[2 * b, :, 384:] + igland[2 * b + 1, :, :128]
@@ -617,15 +612,15 @@
             V((512, 1024), BF), V((512, 1024), BF), V((8, 128, 1024), BF),
             V((2, 4, 128, 512), BF), V((2, 128, 512), BF), V((4, 128, 512), BF), V((4, 128, 512), BF),
             V((4, 128, 512), BF), V((8, 16, 1024), BF), V((8, 16, 1024), BF),
-            V((8, 128, 512), BF), V((8, 512, 128), BF), V((32, 1024), BF), V((16, 32, 1024), BF),
-            V((512, 1024), BF), V((512, 1024), BF), V((1, 1024), F32),
+            V((8, 128, 512), BF), V((512, 1024), BF), V((32, 1024), BF), V((16, 32, 1024), BF),
+            V((512, 1024), BF), V((1, 1024), F32),
             V((4, 128, 1024), BF), V((4, 128, 1024), BF), V((4, 128, 1024), BF), V((4, 128, 1024), BF),
-            V((8, 128, 1024), BF), V((512, 1024), F32), V((8, 1024), F32), V((16, 32, 1024), BF), V((8, 128, 512), BF),
+            V((8, 128, 1024), BF), V((512, 256), F32), V((16, 32, 1024), BF), V((8, 128, 512), BF),
             dma((5,)), dma((2,)), dma((2,)), dma((8,)), dma((16,)), dma((8,)), dma((16,)), dma((8,)), dma((8,)),
             dma((16,)), dma((16,)), dma((8,)), dma((8,)), dma((4,)), dma((4,)), dma((4,)), dma((4,)),
             dma((8,)), dma((8,)), dma((4,)), dma((4,)), dma((1,)), dma((1,)), dma((4,)), dma((4,)),
-            dma((8,)), dma((8,)), dma((4,)), dma((4,)), dma((4,)), dma((4,)), dma((8,)), dma((8,)),
-            dma((32,)), dma((32,)), dma((8,)), dma((8,)), dma((1,)), dma((1,)),
+            dma((8,)), dma((8,)), dma((16,)), dma((16,)), dma((16,)), dma((16,)),
+            dma((64,)), dma((64,)), dma((8,)), dma((8,)),
             pltpu.SemaphoreType.REGULAR, pltpu.SemaphoreType.REGULAR,
         ],
         compiler_params=pltpu.CompilerParams(
@@ -637,8 +632,9 @@
         finish,
         out_shape=(jax.ShapeDtypeStruct((28, 1024), F32), jax.ShapeDtypeStruct((1, 8), F32),
                    jax.ShapeDtypeStruct((1, 1), F32), jax.ShapeDtypeStruct((128, 3584), BF)),
-        in_specs=[vmem, vmem],
+        in_specs=[hbm, hbm],
         out_specs=(vmem, vmem, vmem, vmem),
+        scratch_shapes=[V((16, 32, 1024), BF), V((8, 128, 512), BF), dma((2,))],
         compiler_params=pltpu.CompilerParams(vmem_limit_bytes=32 * 2 ** 20),
     )(wgland, igland)
     return loss.reshape(()), wg, bias.reshape(8), ig

time: 119 us -> 100 us (0.84)
  Pallas kernels: 116 us -> 96.8 us
    pallas_call x1, Pallas kernels: 114 us -> 95.4 us  [on_device(): pl.pallas_call(kernel, out_shape=(jax.ShapeDtypeStruct((16, 32, 1024), BF...]
where the time goes in v4:
time: 100 us; the launch traced here: 99.9 us
  Pallas kernels  96.8 us (97%)
  local copies, waits for them, and re-layouts  2.44 us (2%)
    pallas_call x1, Pallas kernels, on_device(): pl.pallas_call(kernel, out_shape=(jax.ShapeDtypeStruct((16, 32, 1024), BF...  95.4 us
    unnamed x4, local copies, waits for them, and re-layouts  2.44 us

profile of v4, /device:TPU:1, one launch (start us, length us, event | category | flops | bytes accessed | tf_op | source)
XLA Modules:
  0.0 99.9 jit_solution(9796850865009122752)
XLA Ops:
  0.6 95.4 %shard_map.111 = (bf16[16,32,1024]{2,1,0:T(8,128)(2,1)}, bf16[8,128,512]{2,1,0:T(8,128)(2,1)}) custom-call(bf16[8,2,128,512]{3,2,1,0:T(8,128)(2,1)} %bitcast.6, bf16[128,2048]{1,0:T(8,128)(2,1)} %bitcast.7, bf16[512,1024]{1,0:T(8,128)(2,1)} %proj_in.1, s32[8]{0:T(128)} %own_in.1, s32[1,128]{1,0:T(1,128)} %bitcast.8, bf16[128,3584]{1,0:T(8,128)(2,1)} %x_in.1, ...), custom_call_target="tpu_custom_call" | custom-call | flops 8999999488 | bytes 8000000 | tf_op jit(solution)/shard_map/pallas_call | solution.py:604
  96.1 0.0 copy-start
  96.1 1.2 %copy-done = bf16[16,32,1024]{2,1,0:T(8,128)(2,1)S(1)} copy-done((bf16[16,32,1024]{2,1,0:T(8,128)(2,1)S(1)}, bf16[16,32,1024]{2,1,0:T(8,128)(2,1)}, u32[]{:S(2)}) %copy-start) | copy-done | bytes 1048600
  97.3 0.0 copy-start.1
  97.3 1.2 %copy-done.1 = bf16[8,128,512]{2,1,0:T(8,128)(2,1)S(1)} copy-done((bf16[8,128,512]{2,1,0:T(8,128)(2,1)S(1)}, bf16[8,128,512]{2,1,0:T(8,128)(2,1)}, u32[]{:S(2)}) %copy-start.1) | copy-done | bytes 1048600
  98.5 1.4 %shard_map.112 = (f32[28,1024]{1,0:T(8,128)}, f32[1,8]{1,0:T(1,128)}, f32[1,1]{1,0:T(1,128)}, bf16[128,3584]{1,0:T(8,128)(2,1)}) custom-call(bf16[16,32,1024]{2,1,0:T(8,128)(2,1)S(1)} %copy-done, bf16[8,128,512]{2,1,0:T(8,128)(2,1)S(1)} %copy-done.1), custom_call_target="tpu_custom_call" | custom-call | tf_op jit(solution)/shard_map/pallas_call | solution.py:631
Async XLA Ops:
  96.1 1.2 %copy-start = (bf16[16,32,1024]{2,1,0:T(8,128)(2,1)S(1)}, bf16[16,32,1024]{2,1,0:T(8,128)(2,1)}, u32[]{:S(2)}) copy-start(bf16[16,32,1024]{2,1,0:T(8,128)(2,1)} %get-tuple-element.10.wg_in) | copy-start | bytes 3145732
  97.3 1.2 %copy-start.1 = (bf16[8,128,512]{2,1,0:T(8,128)(2,1)S(1)}, bf16[8,128,512]{2,1,0:T(8,128)(2,1)}, u32[]{:S(2)}) copy-start(bf16[8,128,512]{2,1,0:T(8,128)(2,1)} %get-tuple-element.11.ig_in) | copy-start | bytes 3145732

commit v5 on v4

--- a/solution.py
+++ b/solution.py
@@ -24,54 +24,47 @@
     lax.fori_loop(first, last, lambda i, carry: (body(i), carry)[1], 0)
 
 
-def attend(core, c, qo, qs, keys, values, S, mx, acc, out, between):
+def attend(core, c, qo, qs, keys, values, S, mx, acc, out):
+    L = 256 * (c + 1)
     q = jnp.concatenate([r[:, h * 128:(h + 1) * 128] for r in (qo, qs) for h in range(4)], axis=0)
-
-    def score(j, T, masked):
-        at = pl.ds(pl.multiple_of(j * 256, 256), T)
-        if masked:
-            row = lax.broadcasted_iota(jnp.int32, (128, T), 0) + core * 128
-            keep = row >= lax.broadcasted_iota(jnp.int32, (128, T), 1)
-        s_all = lax.dot_general(q, keys[at, :], (((1,), (1,)), ((), ())), preferred_element_type=F32)
+    row = lax.broadcasted_iota(jnp.int32, (128, 256), 0) + core * 128
+    keep = row >= lax.broadcasted_iota(jnp.int32, (128, 256), 1)
+    for a in range(0, L, 512):
+        b = min(a + 512, L)
+        s_all = lax.dot_general(q, keys[a:b, :], (((1,), (1,)), ((), ())), preferred_element_type=F32)
         for h in range(8):
             hr = slice(h * 128, (h + 1) * 128)
             s = s_all[hr]
-            if masked:
-                s = jnp.where(keep, s, -1e30)
-            S[hr, at] = s
-            m = mx[hr, :]
-            for w in range(T // 128):
-                m = jnp.maximum(m, s[:, w * 128:(w + 1) * 128])
-            if masked:
+            if b == L:
+                last = jnp.where(keep, s[:, b - a - 256:], -1e30)
+                s = last if b - a == 256 else jnp.concatenate([s[:, :256], last], axis=1)
+            S[hr, a:b] = s
+            m = s[:, :128]
+            for w in range(128, b - a, 128):
+                m = jnp.maximum(m, s[:, w:w + 128])
+            if a:
+                m = jnp.maximum(mx[hr, :], m)
+            if b == L:
                 m = jnp.broadcast_to(jnp.max(m, axis=1, keepdims=True) * SCALE, (128, 128))
             mx[hr, :] = m
-
-    mx[...] = jnp.full_like(mx, -1e30)
-    loop(0, c // 2, lambda j: score(2 * j, 512, False))
-    loop(0, lax.rem(c, 2), lambda j: score(c - 1, 256, False))
-    score(c, 256, True)
-    acc[...] = jnp.zeros_like(acc)
-    between()
-
-    def weigh(off, W):
-        vt = values[pl.ds(off, W), :]
+    for a in range(0, L, 1024):
+        b = min(a + 1024, L)
+        vt = values[a:b, :]
         vt = jnp.concatenate([vt, jnp.ones_like(vt)], axis=1)
         ps = []
         for h in range(8):
             hr = slice(h * 128, (h + 1) * 128)
             m = mx[hr, :]
             ps.append(jnp.concatenate(
-                [jnp.exp2(S[hr, pl.ds(pl.multiple_of(off + w * 128, 128), 128)] * SCALE - m).astype(BF)
-                 for w in range(W // 128)], axis=1))
-        acc[...] += jnp.dot(jnp.concatenate(ps, axis=0), vt, preferred_element_type=F32)
-
-    n = c + 1
-    loop(0, n // 4, lambda j: weigh(pl.multiple_of(j * 1024, 1024), 1024))
-    loop(0, lax.rem(n // 2, 2), lambda j: weigh(pl.multiple_of(n // 4 * 1024, 512), 512))
-    loop(0, lax.rem(n, 2), lambda j: weigh(pl.multiple_of((n - 1) * 256, 256), 256))
+                [jnp.exp2(S[hr, w:w + 128] * SCALE - m).astype(BF) for w in range(a, b, 128)], axis=1))
+        o = jnp.dot(jnp.concatenate(ps, axis=0), vt, preferred_element_type=F32)
+        if a:
+            o = o + acc[...]
+        if b < L:
+            acc[...] = o
     for h in range(8):
-        a = acc[h * 128:(h + 1) * 128, :]
-        out[:, h * 128:(h + 1) * 128] = (a[:, :128] / a[:, 128:]).astype(BF)
+        r = o[h * 128:(h + 1) * 128]
+        out[:, h * 128:(h + 1) * 128] = (r[:, :128] / r[:, 128:]).astype(BF)
 
 
 def kernel(q_in, kv_in, proj_in, own_in, ids_in, x_in, w_in, b_in,
@@ -290,21 +283,18 @@
             def _():
                 rcopy(xland.at[j], xland.at[j], x_s.at[0], x_r.at[j], g, sib).wait_recv()
 
-
-        def one(i, j, dst):
-            fetch(j)
+        def forward(half, dst):
+            first = half * 4
+            loop(0, 4, lambda i: fetch(first + i))
+            rows = xland[pl.ds(first, 4)].reshape(512, 512)
             for n in range(4):
                 cols = slice(n * 256, (n + 1) * 256)
-                o = jnp.dot(xland[j], wz[:, cols], preferred_element_type=F32) + brow[:, cols]
-                dst[i, :, cols] = o.astype(BF)
-
-        def theirs(i):
-            xx = lax.rem(x + i, 4)
-            one(xx, (1 - core) * 4 + xx, osib)
-            os_send(xx, True)
-
-        loop(0, 4, theirs)
-        loop(0, 4, lambda i: one(i, core * 4 + i, osend))
+                o = jnp.dot(rows, wz[:, cols], preferred_element_type=F32) + brow[:, cols]
+                dst[:, :, cols] = o.astype(BF).reshape(4, 128, 256)
+
+        forward(1 - core, osib)
+        loop(0, 4, lambda i: os_send(i, True))
+        forward(core, osend)
 
     def output_sums():
         def one(i):
@@ -333,15 +323,20 @@
         z = lax.rem(cz + k * (1 + 2 * core), 4)
         c = z * 2 + lax.rem(ch + jnp.where(other, 1, 0), 2)
 
-        @pl.when(i == 4)
+        @pl.when(i == 3)
         def _():
             student_forward()
 
-        @pl.when(i == 6)
+        @pl.when(i == 5)
         def _():
             output_sums()
 
-        attend(core, c, qo.at[c], qs.at[c], keys, values, S, mx, acc, att, lambda: first_chunk(i))
+        first_chunk(i)
+
+        def at(n):
+            return lambda: attend(core, n, qo.at[n], qs.at[n], keys, values, S, mx, acc, att)
+
+        lax.switch(c, [at(n) for n in range(8)])
         for n in range(4):
             cols = slice(n * 256, (n + 1) * 256)
             p = jnp.dot(att[:, :512], proj_o[:, cols], preferred_element_type=F32)
@@ -635,7 +630,7 @@
         in_specs=[hbm, hbm],
         out_specs=(vmem, vmem, vmem, vmem),
         scratch_shapes=[V((16, 32, 1024), BF), V((8, 128, 512), BF), dma((2,))],
-        compiler_params=pltpu.CompilerParams(vmem_limit_bytes=32 * 2 ** 20),
+        compiler_params=pltpu.CompilerParams(vmem_limit_bytes=60 * 2 ** 20),
     )(wgland, igland)
     return loss.reshape(()), wg, bias.reshape(8), ig
 

time: 100 us -> 97.2 us (0.972)
  local copies, waits for them, and re-layouts: 2.44 us -> 0 us
    unnamed x4 -> x0, local copies, waits for them, and re-layouts: 2.44 us -> none
    pallas_call x1, Pallas kernels: 95.4 us -> 93.6 us  [on_device(): pl.pallas_call(kernel, out_shape=(jax.ShapeDtypeStruct((16, 32, 1024), BF...]
    pallas_call x1, Pallas kernels: 1.37 us -> 2.59 us  [on_device(): pl.pallas_call(finish, out_shape=(jax.ShapeDtypeStruct((28, 1024), F32),...]
where the time goes in v5:
time: 97.2 us; the launch traced here: 97 us
  Pallas kernels  96.2 us (99%)
    pallas_call x1, Pallas kernels, on_device(): pl.pallas_call(kernel, out_shape=(jax.ShapeDtypeStruct((16, 32, 1024), BF...  93.6 us
    pallas_call x1, Pallas kernels, on_device(): pl.pallas_call(finish, out_shape=(jax.ShapeDtypeStruct((28, 1024), F32),...  2.59 us

profile of v5, /device:TPU:1, one launch (start us, length us, event | category | flops | bytes accessed | tf_op | source)
XLA Modules:
  0.0 97.0 jit_solution(8141314217260956034)
XLA Ops:
  0.6 93.6 %shard_map.111 = (bf16[16,32,1024]{2,1,0:T(8,128)(2,1)}, bf16[8,128,512]{2,1,0:T(8,128)(2,1)}) custom-call(bf16[8,2,128,512]{3,2,1,0:T(8,128)(2,1)} %bitcast.6, bf16[128,2048]{1,0:T(8,128)(2,1)} %bitcast.7, bf16[512,1024]{1,0:T(8,128)(2,1)} %proj_in.1, s32[8]{0:T(128)} %own_in.1, s32[1,128]{1,0:T(1,128)} %bitcast.8, bf16[128,3584]{1,0:T(8,128)(2,1)} %x_in.1, ...), custom_call_target="tpu_custom_call" | custom-call | flops 8999999488 | bytes 8000000 | tf_op jit(solution)/shard_map/pallas_call | solution.py:599
  94.3 2.6 %shard_map.112 = (f32[28,1024]{1,0:T(8,128)}, f32[1,8]{1,0:T(1,128)}, f32[1,1]{1,0:T(1,128)}, bf16[128,3584]{1,0:T(8,128)(2,1)}) custom-call(bf16[16,32,1024]{2,1,0:T(8,128)(2,1)} %get-tuple-element.10.wg_in, bf16[8,128,512]{2,1,0:T(8,128)(2,1)} %get-tuple-element.11.ig_in), custom_call_target="tpu_custom_call" | custom-call | tf_op jit(solution)/shard_map/pallas_call | solution.py:626

commit v6 on v5

--- a/solution.py
+++ b/solution.py
@@ -84,9 +84,6 @@
     def member(i):
         return yl * 4 + lax.rem(i, 4), chip * 2 + i // 4
 
-    def plane(i):
-        return lax.rem(i, 2) * 4 + x, (i // 2) * 2 + yl
-
     own_kv = pl.ds(pl.multiple_of(t * 128, 128), 128)
     kcol = pl.ds(pl.multiple_of(chip * 128, 128), 128)
     vcol = pl.ds(pl.multiple_of(1024 + chip * 128, 128), 128)
@@ -181,11 +178,11 @@
     pl.semaphore_wait(round2, 12)
     pl.semaphore_signal(round3, inc=1, device_id=(g, sib), device_id_type=MESH)
 
-    def w_send(i, start):
-        i = lax.rem(src16 + i, 16)
-        dg, dt = plane(i)
-        here = (i == src16) & (core == yl)
-
+    cz, ch, y = chip // 2, lax.rem(chip, 2), lax.rem(chip, 2) * 2 + yl
+
+    def w_first(i, start):
+        zz, yy = lax.rem(cz + i * (1 - core), 4), lax.rem(y + i * core, 4)
+        here = (i == 0) & (core == yl)
         if start:
             @pl.when(here)
             def _():
@@ -193,12 +190,57 @@
 
         @pl.when(jnp.logical_not(here))
         def _():
-            copy = rcopy(w_pad, wland.at[t], w_s.at[i], w_r.at[t], dg, dt)
+            copy = rcopy(w_pad, wland.at[t], w_s.at[i], w_r.at[t],
+                         lax.rem(yy, 2) * 4 + x, zz * 4 + yy // 2 * 2 + yl)
             if start:
                 copy.start()
             else:
                 copy.wait_send()
 
+    def w_wait(i):
+        pltpu.make_async_copy(w_pad, wland.at[i], w_r.at[i]).wait()
+
+    def w_along_y(i, start):
+        slot = i * 4 + ch * 2
+        if start:
+            w_wait(slot)
+        for k in range(1, 4):
+            yy = lax.rem(y + k, 4)
+            copy = rcopy(wland.at[slot], wland.at[slot], w_s.at[4 + i * 3 + k - 1], w_r.at[slot],
+                         lax.rem(yy, 2) * 4 + x, cz * 4 + yy // 2 * 2 + core)
+            if start:
+                copy.start()
+            else:
+                copy.wait_send()
+
+    def w_along_z(i, start):
+        slot = cz * 4 + i * 2 + 1
+        if start:
+            w_wait(slot)
+        for k in range(1, 4):
+            zz = lax.rem(cz + k, 4)
+            copy = rcopy(wland.at[slot], wland.at[slot], w_s.at[16 + i * 3 + k - 1], w_r.at[slot],
+                         g, zz * 4 + ch * 2 + core)
+            if start:
+                copy.start()
+            else:
+                copy.wait_send()
+
+    def w_second(start):
+        @pl.when(core == yl)
+        def _():
+            loop(0, 4, lambda i: w_along_y(i, start))
+
+        loop(0, 2, lambda i: w_along_z(i, start))
+
+    def w_late(i):
+        early_y = (lax.rem(i, 2) == 0) & (core == yl) & (lax.rem(i // 2, 2) == ch)
+        early_z = (lax.rem(i, 2) == 1) & (i // 4 == cz)
+
+        @pl.when(jnp.logical_not(early_y | early_z))
+        def _():
+            w_wait(i)
+
     def x_send(i, start):
         j = lax.rem(m + i, 8)
         dg, dt = member(j)
@@ -208,16 +250,16 @@
         else:
             copy.wait_send()
 
+    pl.semaphore_wait(round3, 1)
+    loop(0, 4, lambda i: w_first(i, True))
     loop(1, 8, lambda i: x_send(i, True))
     loop(1, 8, v_pass)
     pcopy.start()
-    pl.semaphore_wait(round3, 1)
-    loop(0, 16, lambda i: w_send(i, True))
+    w_second(True)
     loop(0, 8, lambda i: k_relay(i * 2 + 1 - core).wait_recv())
     local[2].wait()
     qcopy.wait_recv()
 
-    cz, ch = chip // 2, lax.rem(chip, 2)
     A, B = pl.ds(0, 512), pl.ds(512, 512)
 
     def ta_send(c, start):
@@ -267,7 +309,7 @@
     off = pl.multiple_of(lax.rem(x, 2) * 64, 64)
 
     def student_forward():
-        loop(0, 16, lambda i: pltpu.make_async_copy(w_pad, wland.at[i], w_r.at[i]).wait())
+        loop(0, 16, w_late)
         wz[...] = jnp.zeros_like(wz)
         bias = jnp.zeros((1, 1024), F32)
         for a in range(4):
@@ -327,7 +369,7 @@
         def _():
             student_forward()
 
-        @pl.when(i == 5)
+        @pl.when(i == 4)
         def _():
             output_sums()
 
@@ -545,7 +587,8 @@
     pcopy.wait_send()
     loop(0, 8, lambda i: k_relay(i * 2 + core).wait_send())
     loop(0, 8, lambda i: v_relay(i * 2 + core).wait_send())
-    loop(0, 16, lambda i: w_send(i, False))
+    loop(0, 4, lambda i: w_first(i, False))
+    w_second(False)
     loop(1, 8, lambda i: x_send(i, False))
     loop(0, 4, lambda i: os_send(i, False))
     loop(1, 4, lambda i: o_send(i, False))
@@ -612,7 +655,7 @@
             V((4, 128, 1024), BF), V((4, 128, 1024), BF), V((4, 128, 1024), BF), V((4, 128, 1024), BF),
             V((8, 128, 1024), BF), V((512, 256), F32), V((16, 32, 1024), BF), V((8, 128, 512), BF),
             dma((5,)), dma((2,)), dma((2,)), dma((8,)), dma((16,)), dma((8,)), dma((16,)), dma((8,)), dma((8,)),
-            dma((16,)), dma((16,)), dma((8,)), dma((8,)), dma((4,)), dma((4,)), dma((4,)), dma((4,)),
+            dma((22,)), dma((16,)), dma((8,)), dma((8,)), dma((4,)), dma((4,)), dma((4,)), dma((4,)),
             dma((8,)), dma((8,)), dma((4,)), dma((4,)), dma((1,)), dma((1,)), dma((4,)), dma((4,)),
             dma((8,)), dma((8,)), dma((16,)), dma((16,)), dma((16,)), dma((16,)),
             dma((64,)), dma((64,)), dma((8,)), dma((8,)),

time: 97.2 us -> 95.5 us (0.983)
  Pallas kernels: 96.2 us -> 93.8 us
    pallas_call x1, Pallas kernels: 93.6 us -> 91.2 us  [on_device(): pl.pallas_call(kernel, out_shape=(jax.ShapeDtypeStruct((16, 32, 1024), BF...]
where the time goes in v6:
time: 95.5 us; the launch traced here: 94.6 us
  Pallas kernels  93.8 us (98%)
    pallas_call x1, Pallas kernels, on_device(): pl.pallas_call(kernel, out_shape=(jax.ShapeDtypeStruct((16, 32, 1024), BF...  91.2 us
    pallas_call x1, Pallas kernels, on_device(): pl.pallas_call(finish, out_shape=(jax.ShapeDtypeStruct((28, 1024), F32),...  2.59 us

profile of v6, /device:TPU:1, one launch (start us, length us, event | category | flops | bytes accessed | tf_op | source)
XLA Modules:
  0.0 94.6 jit_solution(13205625275980397253)
XLA Ops:
  0.6 91.2 %shard_map.111 = (bf16[16,32,1024]{2,1,0:T(8,128)(2,1)}, bf16[8,128,512]{2,1,0:T(8,128)(2,1)}) custom-call(bf16[8,2,128,512]{3,2,1,0:T(8,128)(2,1)} %bitcast.6, bf16[128,2048]{1,0:T(8,128)(2,1)} %bitcast.7, bf16[512,1024]{1,0:T(8,128)(2,1)} %proj_in.1, s32[8]{0:T(128)} %own_in.1, s32[1,128]{1,0:T(1,128)} %bitcast.8, bf16[128,3584]{1,0:T(8,128)(2,1)} %x_in.1, ...), custom_call_target="tpu_custom_call" | custom-call | flops 8999999488 | bytes 8000000 | tf_op jit(solution)/shard_map/pallas_call | solution.py:642
  91.9 2.6 %shard_map.112 = (f32[28,1024]{1,0:T(8,128)}, f32[1,8]{1,0:T(1,128)}, f32[1,1]{1,0:T(1,128)}, bf16[128,3584]{1,0:T(8,128)(2,1)}) custom-call(bf16[16,32,1024]{2,1,0:T(8,128)(2,1)} %get-tuple-element.10.wg_in, bf16[8,128,512]{2,1,0:T(8,128)(2,1)} %get-tuple-element.11.ig_in), custom_call_target="tpu_custom_call" | custom-call | tf_op jit(solution)/shard_map/pallas_call | solution.py:669

commit v7 on v6

--- a/solution.py
+++ b/solution.py
@@ -506,9 +506,6 @@
                 copy.wait_send()
 
     def weight_grad(n):
-        if n < 3:
-            for k in range(4):
-                e_relay(k, n).wait_recv()
         cols = slice(n * 256, (n + 1) * 256)
         eb = jnp.zeros((8, 256), F32)
         lb = jnp.zeros((8, 256), F32)
@@ -534,12 +531,18 @@
 
     for n in range(4):
         e_begin(n)
-    for n in range(3):
+    def e_done(n):
+        for k in range(4):
+            e_relay(k, n).wait_recv()
+
+    for n in range(2):
         e_pass(n)
+        e_done(n)
         weight_grad(n)
-    e_pass(3)
-    for k in range(4):
-        e_relay(k, 3).wait_recv()
+    for n in (2, 3):
+        e_pass(n)
+    for n in (2, 3):
+        e_done(n)
 
     def i_send(k, j, slot, start):
         dg, dt = member(j)
@@ -552,6 +555,8 @@
     pairs = [(2, wz, m), (1, wz, m), (3, wz, m), (0, wz, m)]
     ig_own = [pltpu.make_async_copy(igsend.at[6], igland.at[m], i_r.at[m])]
     for k, (dx, w, slot) in enumerate(pairs):
+        if k == 2:
+            weight_grad(2)
         if k == 3:
             weight_grad(3)
         xx = lax.rem(x + dx, 4)

time: 95.5 us -> 93.7 us (0.981)
  Pallas kernels: 93.8 us -> 91.9 us
    pallas_call x1, Pallas kernels: 91.2 us -> 89.3 us  [on_device(): pl.pallas_call(kernel, out_shape=(jax.ShapeDtypeStruct((16, 32, 1024), BF...]
where the time goes in v7:
time: 93.7 us; the launch traced here: 92.7 us
  Pallas kernels  91.9 us (98%)
    pallas_call x1, Pallas kernels, on_device(): pl.pallas_call(kernel, out_shape=(jax.ShapeDtypeStruct((16, 32, 1024), BF...  89.3 us
    pallas_call x1, Pallas kernels, on_device(): pl.pallas_call(finish, out_shape=(jax.ShapeDtypeStruct((28, 1024), F32),...  2.59 us

profile of v7, /device:TPU:1, one launch (start us, length us, event | category | flops | bytes accessed | tf_op | source)
XLA Modules:
  0.0 92.7 jit_solution(3355873388281310823)
XLA Ops:
  0.6 89.3 %shard_map.111 = (bf16[16,32,1024]{2,1,0:T(8,128)(2,1)}, bf16[8,128,512]{2,1,0:T(8,128)(2,1)}) custom-call(bf16[8,2,128,512]{3,2,1,0:T(8,128)(2,1)} %bitcast.6, bf16[128,2048]{1,0:T(8,128)(2,1)} %bitcast.7, bf16[512,1024]{1,0:T(8,128)(2,1)} %proj_in.1, s32[8]{0:T(128)} %own_in.1, s32[1,128]{1,0:T(1,128)} %bitcast.8, bf16[128,3584]{1,0:T(8,128)(2,1)} %x_in.1, ...), custom_call_target="tpu_custom_call" | custom-call | flops 8999999488 | bytes 8000000 | tf_op jit(solution)/shard_map/pallas_call | solution.py:647
  89.9 2.6 %shard_map.112 = (f32[28,1024]{1,0:T(8,128)}, f32[1,8]{1,0:T(1,128)}, f32[1,1]{1,0:T(1,128)}, bf16[128,3584]{1,0:T(8,128)(2,1)}) custom-call(bf16[16,32,1024]{2,1,0:T(8,128)(2,1)} %get-tuple-element.10.wg_in, bf16[8,128,512]{2,1,0:T(8,128)(2,1)} %get-tuple-element.11.ig_in), custom_call_target="tpu_custom_call" | custom-call | tf_op jit(solution)/shard_map/pallas_call | solution.py:674

commit v8 on v7

--- a/solution.py
+++ b/solution.py
@@ -530,6 +530,9 @@
         loop(0, 16, lambda i: g_send(lax.rem(t + i, 16), n, True))
 
     for n in range(4):
+        if n >= 2:
+            for dx in (1, 2, 3):
+                e_send(dx, n - 2).wait_send()
         e_begin(n)
     def e_done(n):
         for k in range(4):
@@ -604,7 +607,8 @@
     loop(1, 8, lambda i: p_send(i, False))
     for n in range(4):
         for dx in (1, 2, 3):
-            e_send(dx, n).wait_send()
+            if n >= 2:
+                e_send(dx, n).wait_send()
         for dx in range(4):
             e_relay(dx, n).wait_send()
         loop(0, 16, lambda i: g_send(i, n, False))

time: 93.7 us -> 93.8 us (level)
  no operation moved by 1% of the time
where the time goes in v8:
time: 93.8 us; the launch traced here: 92.7 us
  Pallas kernels  91.9 us (98%)
    pallas_call x1, Pallas kernels, on_device(): pl.pallas_call(kernel, out_shape=(jax.ShapeDtypeStruct((16, 32, 1024), BF...  89.3 us
    pallas_call x1, Pallas kernels, on_device(): pl.pallas_call(finish, out_shape=(jax.ShapeDtypeStruct((28, 1024), F32),...  2.59 us

profile of v8, /device:TPU:1, one launch (start us, length us, event | category | flops | bytes accessed | tf_op | source)
XLA Modules:
  0.0 92.7 jit_solution(12466452383371767720)
XLA Ops:
  0.6 89.3 %shard_map.111 = (bf16[16,32,1024]{2,1,0:T(8,128)(2,1)}, bf16[8,128,512]{2,1,0:T(8,128)(2,1)}) custom-call(bf16[8,2,128,512]{3,2,1,0:T(8,128)(2,1)} %bitcast.6, bf16[128,2048]{1,0:T(8,128)(2,1)} %bitcast.7, bf16[512,1024]{1,0:T(8,128)(2,1)} %proj_in.1, s32[8]{0:T(128)} %own_in.1, s32[1,128]{1,0:T(1,128)} %bitcast.8, bf16[128,3584]{1,0:T(8,128)(2,1)} %x_in.1, ...), custom_call_target="tpu_custom_call" | custom-call | flops 8999999488 | bytes 8000000 | tf_op jit(solution)/shard_map/pallas_call | solution.py:651
  89.9 2.6 %shard_map.112 = (f32[28,1024]{1,0:T(8,128)}, f32[1,8]{1,0:T(1,128)}, f32[1,1]{1,0:T(1,128)}, bf16[128,3584]{1,0:T(8,128)(2,1)}) custom-call(bf16[16,32,1024]{2,1,0:T(8,128)(2,1)} %get-tuple-element.10.wg_in, bf16[8,128,512]{2,1,0:T(8,128)(2,1)} %get-tuple-element.11.ig_in), custom_call_target="tpu_custom_call" | custom-call | tf_op jit(solution)/shard_map/pallas_call | solution.py:678
